TPU v7x, 256 devices: a whole 4x4x8 slice. The times are simulated.
256 devices in a mesh: hid: 32 (over x, y, z_lo), wid: 8 (over z_hi, core).
Axes of the slice: x: 4, y: 4, z: 8 (z_hi: 4, z_lo: 2; z = z_hi * 2 + z_lo), core: 2. Of those that a mesh axis runs over, the one named last changes fastest.
Arguments:
- inputs: bfloat16 [1024, 8192], P('hid', 'wid'), may hold values from -6 to 6
- out_grad: bfloat16 [1024, 8192], P('hid', 'wid'), may hold values from -6 to 6
- gate_pre: bfloat16 [1024, 28672], P('wid', 'hid'), may hold values from -8 to 8
- up_pre: bfloat16 [1024, 28672], P('wid', 'hid'), may hold values from -6 to 6
- w_gate: bfloat16 [8192, 28672], P('wid', 'hid'), may hold values from -0.0625 to 0.0625
- w_up: bfloat16 [8192, 28672], P('wid', 'hid'), may hold values from -0.0625 to 0.0625
- w_down: bfloat16 [28672, 8192], P('hid', 'wid'), may hold values from -0.03125 to 0.03125
Outputs:
- grad_inputs: bfloat16 [1024, 8192], P('hid', 'wid')
- grad_gate: bfloat16 [8192, 28672], P('wid', 'hid')
- grad_up: bfloat16 [8192, 28672], P('wid', 'hid')
- grad_down: bfloat16 [28672, 8192], P('hid', 'wid')
All inputs are finite; a program needn't handle non-finite values.
Results may differ from a plain program's by a relative error of at most 0.0049.
Values may be sent and summed in bfloat16 or wider, within the bound.
No kernel may reach another device: no remote copies, remote signals or barrier semaphores. Data moves between devices by JAX's collectives and lax.ppermute only.
A program may use at most 64 MiB of HBM per device.

v0:
```python
import functools

import jax
import jax.numpy as jnp
from jax import lax
from jax.experimental import pallas as pl
from jax.experimental.pallas import tpu as pltpu
from jax.sharding import PartitionSpec as P

BF = jnp.bfloat16
F32 = jnp.float32
T, DB, FB = 1024, 1024, 896
COL_TILES = ((0, 256), (256, 256), (512, 256), (768, 128))
VMEM = pl.BlockSpec(memory_space=pltpu.VMEM)
ANY = pl.BlockSpec(memory_space=pl.ANY)
HBM = pl.BlockSpec(memory_space=pltpu.HBM)
SMEM = pl.BlockSpec(memory_space=pltpu.SMEM)


def shift_x(value, step):
    return lax.ppermute(value, "hid", [(h, (h + 8 * step) % 32) for h in range(32)])


def shift_y(value, step):
    return lax.ppermute(
        value, "hid", [(h, h // 8 * 8 + (h % 8 + 2 * step) % 8) for h in range(32)]
    )


def swap_x(value, bit):
    return lax.ppermute(value, "hid", [(h, h ^ (8 * bit)) for h in range(32)])


def swap_y(value, bit):
    return lax.ppermute(value, "hid", [(h, h ^ (2 * bit)) for h in range(32)])


def swap_zl(value):
    return lax.ppermute(value, "hid", [(h, h ^ 1) for h in range(32)])


def shift_zh(value, step):
    return lax.ppermute(value, "wid", [(w, (w + 2 * step) % 8) for w in range(8)])


def swap_core(value):
    return lax.ppermute(value, "wid", [(w, w ^ 1) for w in range(8)])


def local_row(pos, bx, by):
    zh, core = pos[3], pos[4]
    return pl.multiple_of(
        ((by // 2) ^ core) * 512 + ((bx - zh) & 3) * 128 + (by & 1) * 64, 64
    )


def to_local(pos, rows, out, place):
    for i in range(rows.shape[0] // 64):
        out[pl.ds(local_row(pos, *place(i)), 64)] = rows[i * 64 : (i + 1) * 64]


def dot_nt(left, right):
    return lax.dot_general(left, right, (((1,), (1,)), ((), ())), preferred_element_type=F32)


def dot_tn(left, right):
    return lax.dot_general(left, right, (((0,), (0,)), ((), ())), preferred_element_type=F32)


def call(kernel, outs, cost, scratch=(), whole=0, after=0, stay=0):
    flops, nbytes = cost

    def body(*refs):
        n = len(refs) - len(outs) - len(scratch)
        kernel(*refs[: n - after], *refs[n:])

    def run(*args):
        plain = len(args) - whole - after
        kept = [
            pltpu.with_memory_space_constraint(arg, pltpu.HBM)
            for arg in args[plain : plain + whole + stay]
        ]
        return pl.pallas_call(
            body,
            out_shape=[(pltpu.HBM if o[2:] else jax.ShapeDtypeStruct)(*o[:2]) for o in outs],
            in_specs=[SMEM] + [VMEM] * (plain - 1) + [HBM] * (whole + stay) + [ANY] * (after - stay),
            out_specs=[HBM if o[2:] else VMEM for o in outs],
            scratch_shapes=list(scratch),
            cost_estimate=pl.CostEstimate(flops=flops, bytes_accessed=nbytes, transcendentals=0),
            compiler_params=pltpu.CompilerParams(vmem_limit_bytes=16 * 2**20),
        )(*args[:plain], *kept, *args[plain + whole + stay :])

    return run


def start_all(copies):
    for copy in copies:
        copy.start()
    return copies


def wait_all(copies):
    for copy in copies:
        copy.wait()


def pair_kernel(pos, other, rows_other, mine, rows_mine, gate, up, out, rows_out, acts_out, sems):
    row = pl.multiple_of(pos[2] * 32, 32)
    other_row = pl.multiple_of(32 - pos[2] * 32, 32)
    moves = [
        (mine, out.at[pl.ds(row, 32)]),
        (other, out.at[pl.ds(other_row, 32)]),
        (rows_mine, rows_out.at[pl.ds(row, 32)]),
        (rows_other, rows_out.at[pl.ds(other_row, 32)]),
        (gate, acts_out.at[pl.ds(0, 128)]),
        (up, acts_out.at[pl.ds(128, 128)]),
    ]
    wait_all(
        start_all([pltpu.make_async_copy(a, b, sems.at[i]) for i, (a, b) in enumerate(moves)])
    )


def rows_kernel(pos, *refs):
    for i, part in enumerate(refs[:4]):
        refs[4][i * 64 : (i + 1) * 64] = part[...]


def hidden_grad_kernel(pos, *refs):
    pieces, (w_down, near, far, grads, keep, send, rows_out) = refs[:4], refs[4:]
    for j, piece in enumerate(pieces):
        to_local(pos, piece, grads, lambda k, j=j: ((pos[0] - k) & 3, (pos[1] - j) & 3))
    for start, width in COL_TILES:
        cols = slice(start, start + width)
        part = dot_nt(grads[...], w_down[cols, :])
        keep[:, cols] = part[:512]
        send[:, cols] = part[512:]
    rows_out[:128] = near[...]
    rows_out[128:] = far[...]


def pair_sum_kernel(pos, keep, got, *refs):
    acts = refs[:5]
    own, one, two, three, acts_out, sems = refs[5:]
    copies = []
    for i, (block, row) in enumerate(zip(acts, (0, 256, 768, 512, 640))):
        place = acts_out.at[pl.ds(row, block.shape[0])]
        copies.append(pltpu.make_async_copy(block, place, sems.at[i]))
    start_all(copies)
    own[...] = keep[:128] + got[:128]
    for k, out in enumerate((one, two, three)):
        rows = slice(128 * (k + 1), 128 * (k + 2))
        out[...] = (keep[rows] + got[rows]).astype(BF)
    wait_all(copies)


def ring_sum_kernel(pos, own, one, two, three, near, far, out, rows_out):
    rows_out[:256] = near[...]
    rows_out[256:] = far[...]
    total = own[...] + one[...].astype(F32) + two[...].astype(F32) + three[...].astype(F32)
    out[...] = total.astype(BF)


def down_kernel(pos, *refs):
    blocks, (grads, out, act_out, slope_out, hidden) = refs[:2], refs[2:]
    for i in range(8):
        rows = slice(i * 128, (i + 1) * 128)
        start = 256 * (i % 4)
        gate = blocks[i // 4][start : start + 128].astype(F32)
        up = blocks[i // 4][start + 128 : start + 256].astype(F32)
        sig = jax.nn.sigmoid(gate)
        act = gate * sig
        act_out[rows] = act
        slope_out[rows] = up * sig * (1.0 + gate * (1.0 - sig))
        hidden[rows] = (act * up).astype(BF)
    for start in range(0, DB, 256):
        cols = slice(start, start + 256)
        out[:, cols] = dot_tn(hidden[...], grads[:, cols]).astype(BF)


def sum_kernel(pos, parts, out):
    total = parts[0].astype(F32)
    for i in range(1, 32):
        total = total + parts[i].astype(F32)
    out[...] = total.astype(BF)


def input_grad_kernel(pos, *refs):
    hgs, (act, slope, w_gate, w_up, out, gate_out, up_out) = refs[:8], refs[8:15]
    gate_grad, up_grad, part, sems = refs[15:]
    for i in range(8):
        rows = slice(i * 128, (i + 1) * 128)
        hg = hgs[i][...].astype(F32)
        gate_grad[rows] = (hg * slope[rows]).astype(BF)
        up_grad[rows] = (hg * act[rows]).astype(BF)
    copies = start_all(
        [
            pltpu.make_async_copy(gate_grad, gate_out, sems.at[4]),
            pltpu.make_async_copy(up_grad, up_out, sems.at[5]),
        ]
    )
    zh, core = pos[3], pos[4]
    for n, start in enumerate(range(0, DB, 256)):
        cols = slice(start, start + 256)
        block = dot_nt(gate_grad[...], w_gate[cols, :]) + dot_nt(up_grad[...], w_up[cols, :])
        block = block.astype(BF)
        for i in range(8):
            bx = (zh + i % 4) & 3
            by = 2 * ((i // 4) ^ core)
            row = pl.multiple_of(bx * 256 + by * 64, 128)
            part[n, pl.ds(row, 128)] = block[i * 128 : (i + 1) * 128]
        copies += start_all([pltpu.make_async_copy(part.at[n], out.at[:, cols], sems.at[n])])
    wait_all(copies)


def weight_grad_kernel(pos, *refs):
    near, far, gate_grad, up_grad, out_gate, out_up, inputs = refs
    for first, rows in ((0, near), (8, far)):

        def place(i, first=first):
            i += first
            return (i >> 1 & 1 | i >> 2 & 2) ^ pos[0], (i & 1 | i >> 1 & 2) ^ pos[1]

        to_local(pos, rows, inputs, place)
    for start, width in COL_TILES:
        cols = slice(start, start + width)
        out_gate[:, cols] = dot_tn(inputs[...], gate_grad[:, cols]).astype(BF)
        out_up[:, cols] = dot_tn(inputs[...], up_grad[:, cols]).astype(BF)


MM = 2 * T * DB * FB
MB = 2**20
LONG = (12 * MM, 80 * MB)
SHORT = (0, 0)


def spread_core(mine):
    return list(mine) + [swap_core(p) for p in mine]


def gather_zh(block):
    got = [shift_zh(block, k) for k in (1, 2, 3)]
    return [block, got[2], got[1], got[0]]


def ring_zh(block):
    above, below = shift_zh(block, 1), shift_zh(block, 3)
    return [block, below, above, shift_zh(above[:128], 1), shift_zh(below[128:], 3)]


def per_device(inputs, out_grad, gate_pre, up_pre, w_gate, w_up, w_down):
    h, w = lax.axis_index("hid"), lax.axis_index("wid")
    pos = jnp.stack([h // 8, h // 2 % 4, h % 2, w // 2, w % 2]).astype(jnp.int32)

    block, near, acts = call(
        pair_kernel,
        [((64, DB), BF), ((64, DB), BF), ((256, FB), BF)],
        SHORT,
        [pltpu.SemaphoreType.DMA((6,))],
        whole=4,
    )(pos, swap_zl(out_grad), swap_zl(inputs), out_grad, inputs, gate_pre, up_pre)
    acts = ring_zh(acts)
    (block,) = call(rows_kernel, [((256, DB), BF)], (0, MB))(
        pos, block, *[shift_x(block, k) for k in (1, 2, 3)]
    )
    near = jnp.concatenate([near, swap_y(near, 1)])
    far = swap_x(near, 1)
    all_grads, keep, send, near = call(
        hidden_grad_kernel,
        [((T, DB), BF), ((512, FB), F32), ((512, FB), F32), ((256, DB), BF)],
        LONG,
        after=2,
    )(pos, block, *[shift_y(block, k) for k in (1, 2, 3)], w_down, near, far, *acts[3:])
    far = swap_y(near, 2)
    own, one, two, three, acts = call(
        pair_sum_kernel,
        [((128, FB), F32)] + [((128, FB), BF)] * 3 + [((T, FB), BF)],
        LONG,
        [pltpu.SemaphoreType.DMA((5,))],
        whole=5,
    )(pos, keep, swap_core(send), *acts)
    got = [shift_zh(one, 1), shift_zh(two, 2), shift_zh(three, 3)]
    grad_down, act, slope = call(
        down_kernel,
        [((FB, DB), BF), ((T, FB), F32), ((T, FB), F32)],
        (MM, 16 * MB),
        [pltpu.VMEM((T, FB), BF)],
    )(pos, acts, swap_core(acts), all_grads)
    hg, near = call(
        ring_sum_kernel, [((128, FB), BF), ((512, DB), BF)], LONG, after=1
    )(pos, own, *got, near, far, act)
    far = swap_x(near, 2)
    hgs = spread_core(gather_zh(hg))
    partial, gate_grad, up_grad = call(
        input_grad_kernel,
        [((T, DB), BF, HBM), ((T, FB), BF, HBM), ((T, FB), BF, HBM)],
        (2 * MM, 15 * MB),
        [
            pltpu.VMEM((T, FB), BF),
            pltpu.VMEM((T, FB), BF),
            pltpu.VMEM((4, T, 256), BF),
            pltpu.SemaphoreType.DMA((6,)),
        ],
        after=1,
    )(pos, *hgs, act, slope, w_gate, w_up, far)
    parts = lax.all_to_all(partial, "hid", split_axis=0, concat_axis=0, tiled=True)
    (grad_inputs,) = call(sum_kernel, [((32, DB), BF)], (MB, 2 * MB))(
        pos, parts.reshape(32, 32, DB)
    )
    grad_gate, grad_up = call(
        weight_grad_kernel,
        [((DB, FB), BF), ((DB, FB), BF)],
        (2 * MM, 10 * MB),
        [pltpu.VMEM((T, DB), BF)],
    )(pos, near, far, gate_grad, up_grad)
    return (grad_inputs, grad_gate, grad_up, grad_down)


def solution(mesh):
    in_specs = (
        P("hid", "wid"),
        P("hid", "wid"),
        P("wid", "hid"),
        P("wid", "hid"),
        P("wid", "hid"),
        P("wid", "hid"),
        P("hid", "wid"),
    )
    out_specs = (P("hid", "wid"), P("wid", "hid"), P("wid", "hid"), P("hid", "wid"))
    return jax.shard_map(
        per_device, mesh=mesh, in_specs=in_specs, out_specs=out_specs, check_vma=False
    )
```

profile of v0, /device:TPU:64, one launch (start us, length us, event | category | flops | bytes accessed | tf_op | source)
XLA Modules:
  0.0 165.8 jit_solution(1461611853581259447)
XLA Ops:
  2.8 2.6 %collective-permute-done.1.refs_2_ = bf16[32,1024]{1,0:T(8,128)(2,1)S(1)} collective-permute-done((bf16[32,1024]{1,0:T(8,128)(2,1)}, bf16[32,1024]{1,0:T(8,128)(2,1)S(1)}, u32[]{:S(2)}, u32[]{:S(2)}) %collective-permute-start.1) | collective-permute-done | bytes 65568 | tf_op jit(solution)/shard_map/ppermute | solution.py:39
  9.2 2.7 %collective-permute-start.4 = (bf16[64,1024]{1,0:T(8,128)(2,1)S(1)}, bf16[64,1024]{1,0:T(8,128)(2,1)S(1)}, u32[]{:S(2)}, u32[]{:S(2)}) collective-permute-start(bf16[64,1024]{1,0:T(8,128)(2,1)S(1)} %get-tuple-element.26.refs_1_), channel_id=1, source_target_pairs={{0,192},{8,200},{16,208},{24,216},{32,224},{40,232},{48,240},{56,2... | collective-permute-start | bytes 393224 | tf_op jit(solution)/shard_map/ppermute | solution.py:21
  16.3 4.1 %collective-permute-start.10 = (bf16[256,896]{1,0:T(8,128)(2,1)S(1)}, bf16[256,896]{1,0:T(8,128)(2,1)S(1)}, u32[]{:S(2)}, u32[]{:S(2)}) collective-permute-start(bf16[256,896]{1,0:T(8,128)(2,1)S(1)} %get-tuple-element.28.refs_3_), channel_id=1, source_target_pairs={{0,2},{1,3},{2,4},{3,5},{4,6},{5,7},{6,0},{7,1},{8,10},{9,11},{10,... | collective-permute-start | bytes 1376264 | tf_op jit(solution)/shard_map/ppermute | solution.py:43
  21.0 3.1 %collective-permute-start.7 = (bf16[256,1024]{1,0:T(8,128)(2,1)S(1)}, bf16[256,1024]{1,0:T(8,128)(2,1)S(1)}, u32[]{:S(2)}, u32[]{:S(2)}) collective-permute-start(bf16[256,1024]{1,0:T(8,128)(2,1)S(1)} %shard_map.103.refs_1_), channel_id=1, source_target_pairs={{0,48},{8,56},{16,0},{24,8},{32,16},{40,24},{48,32},{56,40},{64,11... | collective-permute-start | bytes 1572872 | tf_op jit(solution)/shard_map/ppermute | solution.py:25
  25.8 6.5 %collective-permute-done.12.refs_4_ = bf16[256,896]{1,0:T(8,128)(2,1)S(1)} collective-permute-done((bf16[256,896]{1,0:T(8,128)(2,1)S(1)}, bf16[256,896]{1,0:T(8,128)(2,1)S(1)}, u32[]{:S(2)}, u32[]{:S(2)}) %collective-permute-start.12) | collective-permute-done | bytes 458784 | tf_op jit(solution)/shard_map/ppermute | solution.py:43
  33.8 8.0 %collective-permute-start.13 = (bf16[128,896]{1,0:T(8,128)(2,1)S(1)}, bf16[128,896]{1,0:T(8,128)(2,1)S(1)}, u32[]{:S(2)}, u32[]{:S(2)}) collective-permute-start(bf16[128,896]{1,0:T(8,128)(2,1)S(1)} %slice.9), channel_id=1, source_target_pairs={{0,6},{1,7},{2,0},{3,1},{4,2},{5,3},{6,4},{7,5},{8,14},{9,15},{10,... | collective-permute-start | bytes 688136 | tf_op jit(solution)/shard_map/ppermute | solution.py:43
  43.6 3.7 %collective-permute-done.5.refs_2_ = bf16[256,1024]{1,0:T(8,128)(2,1)S(1)} collective-permute-done((bf16[256,1024]{1,0:T(8,128)(2,1)S(1)}, bf16[256,1024]{1,0:T(8,128)(2,1)S(1)}, u32[]{:S(2)}, u32[]{:S(2)}) %collective-permute-start.5) | collective-permute-done | bytes 524320 | tf_op jit(solution)/shard_map/ppermute | solution.py:25
  49.5 3.0 %shard_map.104 = (bf16[1024,1024]{1,0:T(8,128)(2,1)S(1)}, f32[512,896]{1,0:T(8,128)S(1)}, f32[512,896]{1,0:T(8,128)S(1)}, bf16[256,1024]{1,0:T(8,128)(2,1)S(1)}) custom-call(s32[5]{0:T(128)S(1)} %stack.23.refs_0_, bf16[256,1024]{1,0:T(8,128)(2,1)S(1)} %shard_map.103.refs_1_, bf16[256,1024]{1,0:T(8,128)(2,1)S(1)} %collective-permute-done.5.refs_2_, ...), custom_call_target="tpu_custom_call" | custom-call | flops 22548578304 | bytes 83886080 | tf_op jit(solution)/shard_map/pallas_call | solution.py:83
  52.7 3.8 %collective-permute-done.14.refs_2_ = f32[512,896]{1,0:T(8,128)S(1)} collective-permute-done((f32[512,896]{1,0:T(8,128)S(1)}, f32[512,896]{1,0:T(8,128)S(1)}, u32[]{:S(2)}, u32[]{:S(2)}) %collective-permute-start.14) | collective-permute-done | bytes 1835040 | tf_op jit(solution)/shard_map/ppermute | solution.py:47
  58.9 5.5 %collective-permute-start.18 = (bf16[256,1024]{1,0:T(8,128)(2,1)S(1)}, bf16[256,1024]{1,0:T(8,128)(2,1)S(1)}, u32[]{:S(2)}, u32[]{:S(2)}) collective-permute-start(bf16[256,1024]{1,0:T(8,128)(2,1)S(1)} %get-tuple-element.35.refs_5_), channel_id=1, source_target_pairs={{0,32},{8,40},{16,48},{24,56},{32,0},{40,8},{48,16},{56,24},{64,96... | collective-permute-start | bytes 1572872 | tf_op jit(solution)/shard_map/ppermute | solution.py:35
  65.4 3.8 %collective-permute-start.16 = (bf16[128,896]{1,0:T(8,128)(2,1)S(1)}, bf16[128,896]{1,0:T(8,128)(2,1)S(1)}, u32[]{:S(2)}, u32[]{:S(2)}) collective-permute-start(bf16[128,896]{1,0:T(8,128)(2,1)S(1)} %get-tuple-element.33), channel_id=1, source_target_pairs={{0,4},{1,5},{2,6},{3,7},{4,0},{5,1},{6,2},{7,3},{8,12},{9,13},{10,... | collective-permute-start | bytes 688136 | tf_op jit(solution)/shard_map/ppermute | solution.py:43
  69.3 4.8 %shard_map.106 = (bf16[896,1024]{1,0:T(8,128)(2,1)}, f32[1024,896]{1,0:T(8,128)S(1)}, f32[1024,896]{1,0:T(8,128)S(1)}) custom-call(s32[5]{0:T(128)S(1)} %stack.23.refs_0_, bf16[1024,896]{1,0:T(8,128)(2,1)S(1)} %get-tuple-element.36.refs_1_, bf16[1024,896]{1,0:T(8,128)(2,1)S(1)} %collective-permute-done.19.refs_2_, ...), custom_call_target="tpu_custom_call" | custom-call | flops 1879048192 | bytes 16777216 | tf_op jit(solution)/shard_map/pallas_call | solution.py:83
  74.1 2.7 %collective-permute-done.18.refs_6_ = bf16[256,1024]{1,0:T(8,128)(2,1)S(1)} collective-permute-done((bf16[256,1024]{1,0:T(8,128)(2,1)S(1)}, bf16[256,1024]{1,0:T(8,128)(2,1)S(1)}, u32[]{:S(2)}, u32[]{:S(2)}) %collective-permute-start.18) | collective-permute-done | bytes 524320 | tf_op jit(solution)/shard_map/ppermute | solution.py:35
  76.9 12.7 %collective-permute-done.16.refs_3_ = bf16[128,896]{1,0:T(8,128)(2,1)S(1)} collective-permute-done((bf16[128,896]{1,0:T(8,128)(2,1)S(1)}, bf16[128,896]{1,0:T(8,128)(2,1)S(1)}, u32[]{:S(2)}, u32[]{:S(2)}) %collective-permute-start.16) | collective-permute-done | bytes 229408 | tf_op jit(solution)/shard_map/ppermute | solution.py:43
  89.6 2.1 %collective-permute-done.17.refs_4_ = bf16[128,896]{1,0:T(8,128)(2,1)S(1)} collective-permute-done((bf16[128,896]{1,0:T(8,128)(2,1)S(1)}, bf16[128,896]{1,0:T(8,128)(2,1)S(1)}, u32[]{:S(2)}, u32[]{:S(2)}) %collective-permute-start.17) | collective-permute-done | bytes 229408 | tf_op jit(solution)/shard_map/ppermute | solution.py:43
  93.9 3.3 %collective-permute-start.22 = (bf16[128,896]{1,0:T(8,128)(2,1)S(1)}, bf16[128,896]{1,0:T(8,128)(2,1)S(1)}, u32[]{:S(2)}, u32[]{:S(2)}) collective-permute-start(bf16[128,896]{1,0:T(8,128)(2,1)S(1)} %get-tuple-element.39.refs_1_), channel_id=1, source_target_pairs={{0,2},{1,3},{2,4},{3,5},{4,6},{5,7},{6,0},{7,1},{8,10},{9,11},{10,... | collective-permute-start | bytes 688136 | tf_op jit(solution)/shard_map/ppermute | solution.py:43
  98.0 2.2 %collective-permute-start.20 = (bf16[128,896]{1,0:T(8,128)(2,1)S(1)}, bf16[128,896]{1,0:T(8,128)(2,1)S(1)}, u32[]{:S(2)}, u32[]{:S(2)}) collective-permute-start(bf16[128,896]{1,0:T(8,128)(2,1)S(1)} %get-tuple-element.39.refs_1_), channel_id=1, source_target_pairs={{0,6},{1,7},{2,0},{3,1},{4,2},{5,3},{6,4},{7,5},{8,14},{9,15},{10,... | collective-permute-start | bytes 688136 | tf_op jit(solution)/shard_map/ppermute | solution.py:43
  100.2 5.1 %collective-permute-done.22.refs_4_ = bf16[128,896]{1,0:T(8,128)(2,1)S(1)} collective-permute-done((bf16[128,896]{1,0:T(8,128)(2,1)S(1)}, bf16[128,896]{1,0:T(8,128)(2,1)S(1)}, u32[]{:S(2)}, u32[]{:S(2)}) %collective-permute-start.22) | collective-permute-done | bytes 229408 | tf_op jit(solution)/shard_map/ppermute | solution.py:43
  105.3 8.1 %collective-permute-done.21.refs_3_ = bf16[128,896]{1,0:T(8,128)(2,1)S(1)} collective-permute-done((bf16[128,896]{1,0:T(8,128)(2,1)S(1)}, bf16[128,896]{1,0:T(8,128)(2,1)S(1)}, u32[]{:S(2)}, u32[]{:S(2)}) %collective-permute-start.21) | collective-permute-done | bytes 229408 | tf_op jit(solution)/shard_map/ppermute | solution.py:43
  113.3 3.1 %collective-permute-done.20.refs_2_ = bf16[128,896]{1,0:T(8,128)(2,1)S(1)} collective-permute-done((bf16[128,896]{1,0:T(8,128)(2,1)S(1)}, bf16[128,896]{1,0:T(8,128)(2,1)S(1)}, u32[]{:S(2)}, u32[]{:S(2)}) %collective-permute-start.20) | collective-permute-done | bytes 229408 | tf_op jit(solution)/shard_map/ppermute | solution.py:43
  117.9 6.2 %shard_map.108 = (bf16[1024,1024]{1,0:T(8,128)(2,1)}, bf16[1024,896]{1,0:T(8,128)(2,1)}, bf16[1024,896]{1,0:T(8,128)(2,1)}) custom-call(s32[5]{0:T(128)S(1)} %stack.23.refs_0_, bf16[128,896]{1,0:T(8,128)(2,1)S(1)} %get-tuple-element.39.refs_1_, bf16[128,896]{1,0:T(8,128)(2,1)S(1)} %collective-permute-done.20.refs_2_, ...), custom_call_target="tpu_custom_call" | custom-call | flops 3758096384 | bytes 15728640 | tf_op jit(solution)/shard_map/pallas_call | solution.py:83
  124.2 7.6 %all-to-all-start = ((bf16[32,32,1024]{2,1,0:T(8,128)(2,1)}), bf16[32,32,1024]{2,1,0:T(8,128)(2,1)S(1)}, u32[]{:S(2)}, u32[]{:S(2)}) async-start(bf16[32,32,1024]{2,1,0:T(8,128)(2,1)} %bitcast.6), calls=%async_computation | async-start | bytes 4194304 | tf_op jit(solution)/shard_map/all_to_all | solution.py:305
  136.1 7.1 %shard_map.110 = (bf16[1024,896]{1,0:T(8,128)(2,1)}, bf16[1024,896]{1,0:T(8,128)(2,1)}) custom-call(s32[5]{0:T(128)S(1)} %stack.23.refs_0_, bf16[512,1024]{1,0:T(8,128)(2,1)S(1)} %get-tuple-element.41.refs_1_, bf16[512,1024]{1,0:T(8,128)(2,1)S(1)} %copy-done.4, bf16[1024,896]{1,0:T(8,128)(2,1)S(1)} %copy-done.8, bf16[1024,896]{1,0:T(8,128)(2,1)S(1)} %copy-done.9), custom_call_target="tpu_custom_call" | custom-call | flops 3758096384 | bytes 10485760 | tf_op jit(solution)/shard_map/pallas_call | solution.py:83
  143.2 21.2 %all-to-all-done.refs_1_ = bf16[32,32,1024]{2,1,0:T(8,128)(2,1)S(1)} async-done(((bf16[32,32,1024]{2,1,0:T(8,128)(2,1)}), bf16[32,32,1024]{2,1,0:T(8,128)(2,1)S(1)}, u32[]{:S(2)}, u32[]{:S(2)}) %all-to-all-start) | async-done | bytes 2097184 | tf_op jit(solution)/shard_map/all_to_all | solution.py:305
  (72 shorter events, 31.7 us)
Async XLA Ops:
  9.0 23.3 %collective-permute-start.12 = (bf16[256,896]{1,0:T(8,128)(2,1)S(1)}, bf16[256,896]{1,0:T(8,128)(2,1)S(1)}, u32[]{:S(2)}, u32[]{:S(2)}) collective-permute-start(bf16[256,896]{1,0:T(8,128)(2,1)S(1)} %get-tuple-element.28.refs_3_), channel_id=1, source_target_pairs={{0,6},{1,7},{2,0},{3,1},{4,2},{5,3},{6,4},{7,5},{8,14},{9,15},{10,... | collective-permute-start | bytes 1376264 | tf_op jit(solution)/shard_map/ppermute | solution.py:43
  9.2 7.1 %collective-permute-start.4 = (bf16[64,1024]{1,0:T(8,128)(2,1)S(1)}, bf16[64,1024]{1,0:T(8,128)(2,1)S(1)}, u32[]{:S(2)}, u32[]{:S(2)}) collective-permute-start(bf16[64,1024]{1,0:T(8,128)(2,1)S(1)} %get-tuple-element.26.refs_1_), channel_id=1, source_target_pairs={{0,192},{8,200},{16,208},{24,216},{32,224},{40,232},{48,240},{56,2... | collective-permute-start | bytes 393224 | tf_op jit(solution)/shard_map/ppermute | solution.py:21
  11.9 8.5 %collective-permute-start.3 = (bf16[64,1024]{1,0:T(8,128)(2,1)S(1)}, bf16[64,1024]{1,0:T(8,128)(2,1)S(1)}, u32[]{:S(2)}, u32[]{:S(2)}) collective-permute-start(bf16[64,1024]{1,0:T(8,128)(2,1)S(1)} %get-tuple-element.26.refs_1_), channel_id=1, source_target_pairs={{0,128},{8,136},{16,144},{24,152},{32,160},{40,168},{48,176},{56,1... | collective-permute-start | bytes 393224 | tf_op jit(solution)/shard_map/ppermute | solution.py:21
  12.7 7.7 %collective-permute-start.2 = (bf16[64,1024]{1,0:T(8,128)(2,1)S(1)}, bf16[64,1024]{1,0:T(8,128)(2,1)S(1)}, u32[]{:S(2)}, u32[]{:S(2)}) collective-permute-start(bf16[64,1024]{1,0:T(8,128)(2,1)S(1)} %get-tuple-element.26.refs_1_), channel_id=1, source_target_pairs={{0,64},{8,72},{16,80},{24,88},{32,96},{40,104},{48,112},{56,120},{... | collective-permute-start | bytes 393224 | tf_op jit(solution)/shard_map/ppermute | solution.py:21
  13.6 11.2 %collective-permute-start.8 = (bf16[64,1024]{1,0:T(8,128)(2,1)S(1)}, bf16[64,1024]{1,0:T(8,128)(2,1)S(1)}, u32[]{:S(2)}, u32[]{:S(2)}) collective-permute-start(bf16[64,1024]{1,0:T(8,128)(2,1)S(1)} %get-tuple-element.27), channel_id=1, source_target_pairs={{0,16},{8,24},{16,0},{24,8},{32,48},{40,56},{48,32},{56,40},{64,80... | collective-permute-start | bytes 393224 | tf_op jit(solution)/shard_map/ppermute | solution.py:35
  16.3 17.4 %collective-permute-start.10 = (bf16[256,896]{1,0:T(8,128)(2,1)S(1)}, bf16[256,896]{1,0:T(8,128)(2,1)S(1)}, u32[]{:S(2)}, u32[]{:S(2)}) collective-permute-start(bf16[256,896]{1,0:T(8,128)(2,1)S(1)} %get-tuple-element.28.refs_3_), channel_id=1, source_target_pairs={{0,2},{1,3},{2,4},{3,5},{4,6},{5,7},{6,0},{7,1},{8,10},{9,11},{10,... | collective-permute-start | bytes 1376264 | tf_op jit(solution)/shard_map/ppermute | solution.py:43
  21.0 22.6 %collective-permute-start.7 = (bf16[256,1024]{1,0:T(8,128)(2,1)S(1)}, bf16[256,1024]{1,0:T(8,128)(2,1)S(1)}, u32[]{:S(2)}, u32[]{:S(2)}) collective-permute-start(bf16[256,1024]{1,0:T(8,128)(2,1)S(1)} %shard_map.103.refs_1_), channel_id=1, source_target_pairs={{0,48},{8,56},{16,0},{24,8},{32,16},{40,24},{48,32},{56,40},{64,11... | collective-permute-start | bytes 1572872 | tf_op jit(solution)/shard_map/ppermute | solution.py:25
  24.1 19.5 %collective-permute-start.6 = (bf16[256,1024]{1,0:T(8,128)(2,1)S(1)}, bf16[256,1024]{1,0:T(8,128)(2,1)S(1)}, u32[]{:S(2)}, u32[]{:S(2)}) collective-permute-start(bf16[256,1024]{1,0:T(8,128)(2,1)S(1)} %shard_map.103.refs_1_), channel_id=1, source_target_pairs={{0,32},{8,40},{16,48},{24,56},{32,0},{40,8},{48,16},{56,24},{64,96... | collective-permute-start | bytes 1572872 | tf_op jit(solution)/shard_map/ppermute | solution.py:25
  24.8 22.5 %collective-permute-start.5 = (bf16[256,1024]{1,0:T(8,128)(2,1)S(1)}, bf16[256,1024]{1,0:T(8,128)(2,1)S(1)}, u32[]{:S(2)}, u32[]{:S(2)}) collective-permute-start(bf16[256,1024]{1,0:T(8,128)(2,1)S(1)} %shard_map.103.refs_1_), channel_id=1, source_target_pairs={{0,16},{8,24},{16,32},{24,40},{32,48},{40,56},{48,0},{56,8},{64,80... | collective-permute-start | bytes 1572872 | tf_op jit(solution)/shard_map/ppermute | solution.py:25
  32.2 9.6 %collective-permute-start.9 = (bf16[128,1024]{1,0:T(8,128)(2,1)S(1)}, bf16[128,1024]{1,0:T(8,128)(2,1)S(1)}, u32[]{:S(2)}, u32[]{:S(2)}) collective-permute-start(bf16[128,1024]{1,0:T(8,128)(2,1)S(1)} %constant_dynamic-update-slice_fusion.refs_6_), channel_id=1, source_target_pairs={{0,64},{8,72},{16,80},{24,88},{32,96},{40,104},{48,112},{56,120},{... | collective-permute-start | bytes 786440 | tf_op jit(solution)/shard_map/ppermute | solution.py:31
  33.8 15.3 %collective-permute-start.13 = (bf16[128,896]{1,0:T(8,128)(2,1)S(1)}, bf16[128,896]{1,0:T(8,128)(2,1)S(1)}, u32[]{:S(2)}, u32[]{:S(2)}) collective-permute-start(bf16[128,896]{1,0:T(8,128)(2,1)S(1)} %slice.9), channel_id=1, source_target_pairs={{0,6},{1,7},{2,0},{3,1},{4,2},{5,3},{6,4},{7,5},{8,14},{9,15},{10,... | collective-permute-start | bytes 688136 | tf_op jit(solution)/shard_map/ppermute | solution.py:43
  41.8 7.7 %collective-permute-start.11 = (bf16[128,896]{1,0:T(8,128)(2,1)S(1)}, bf16[128,896]{1,0:T(8,128)(2,1)S(1)}, u32[]{:S(2)}, u32[]{:S(2)}) collective-permute-start(bf16[128,896]{1,0:T(8,128)(2,1)S(1)} %slice.8), channel_id=1, source_target_pairs={{0,2},{1,3},{2,4},{3,5},{4,6},{5,7},{6,0},{7,1},{8,10},{9,11},{10,... | collective-permute-start | bytes 688136 | tf_op jit(solution)/shard_map/ppermute | solution.py:43
  58.5 10.8 %collective-permute-start.19 = (bf16[1024,896]{1,0:T(8,128)(2,1)S(1)}, bf16[1024,896]{1,0:T(8,128)(2,1)S(1)}, u32[]{:S(2)}, u32[]{:S(2)}) collective-permute-start(bf16[1024,896]{1,0:T(8,128)(2,1)S(1)} %get-tuple-element.36.refs_1_), channel_id=1, source_target_pairs={{0,1},{1,0},{2,3},{3,2},{4,5},{5,4},{6,7},{7,6},{8,9},{9,8},{10,11... | collective-permute-start | bytes 5505032 | tf_op jit(solution)/shard_map/ppermute | solution.py:47
  58.9 18.0 %collective-permute-start.18 = (bf16[256,1024]{1,0:T(8,128)(2,1)S(1)}, bf16[256,1024]{1,0:T(8,128)(2,1)S(1)}, u32[]{:S(2)}, u32[]{:S(2)}) collective-permute-start(bf16[256,1024]{1,0:T(8,128)(2,1)S(1)} %get-tuple-element.35.refs_5_), channel_id=1, source_target_pairs={{0,32},{8,40},{16,48},{24,56},{32,0},{40,8},{48,16},{56,24},{64,96... | collective-permute-start | bytes 1572872 | tf_op jit(solution)/shard_map/ppermute | solution.py:35
  64.4 12.4 %collective-permute-start.15 = (bf16[128,896]{1,0:T(8,128)(2,1)S(1)}, bf16[128,896]{1,0:T(8,128)(2,1)S(1)}, u32[]{:S(2)}, u32[]{:S(2)}) collective-permute-start(bf16[128,896]{1,0:T(8,128)(2,1)S(1)} %get-tuple-element.32), channel_id=1, source_target_pairs={{0,2},{1,3},{2,4},{3,5},{4,6},{5,7},{6,0},{7,1},{8,10},{9,11},{10,... | collective-permute-start | bytes 688136 | tf_op jit(solution)/shard_map/ppermute | solution.py:43
  65.4 24.1 %collective-permute-start.16 = (bf16[128,896]{1,0:T(8,128)(2,1)S(1)}, bf16[128,896]{1,0:T(8,128)(2,1)S(1)}, u32[]{:S(2)}, u32[]{:S(2)}) collective-permute-start(bf16[128,896]{1,0:T(8,128)(2,1)S(1)} %get-tuple-element.33), channel_id=1, source_target_pairs={{0,4},{1,5},{2,6},{3,7},{4,0},{5,1},{6,2},{7,3},{8,12},{9,13},{10,... | collective-permute-start | bytes 688136 | tf_op jit(solution)/shard_map/ppermute | solution.py:43
  69.3 22.4 %collective-permute-start.17 = (bf16[128,896]{1,0:T(8,128)(2,1)S(1)}, bf16[128,896]{1,0:T(8,128)(2,1)S(1)}, u32[]{:S(2)}, u32[]{:S(2)}) collective-permute-start(bf16[128,896]{1,0:T(8,128)(2,1)S(1)} %get-tuple-element.34), channel_id=1, source_target_pairs={{0,6},{1,7},{2,0},{3,1},{4,2},{5,3},{6,4},{7,5},{8,14},{9,15},{10,... | collective-permute-start | bytes 688136 | tf_op jit(solution)/shard_map/ppermute | solution.py:43
  92.4 25.5 %collective-permute-start.27 = (bf16[512,1024]{1,0:T(8,128)(2,1)S(1)}, bf16[512,1024]{1,0:T(8,128)(2,1)S(1)}, u32[]{:S(2)}, u32[]{:S(2)}) collective-permute-start(bf16[512,1024]{1,0:T(8,128)(2,1)S(1)} %get-tuple-element.41.refs_1_), channel_id=1, source_target_pairs={{0,128},{8,136},{16,144},{24,152},{32,160},{40,168},{48,176},{56,1... | collective-permute-start | bytes 3145736 | tf_op jit(solution)/shard_map/ppermute | solution.py:31
  93.9 11.3 %collective-permute-start.22 = (bf16[128,896]{1,0:T(8,128)(2,1)S(1)}, bf16[128,896]{1,0:T(8,128)(2,1)S(1)}, u32[]{:S(2)}, u32[]{:S(2)}) collective-permute-start(bf16[128,896]{1,0:T(8,128)(2,1)S(1)} %get-tuple-element.39.refs_1_), channel_id=1, source_target_pairs={{0,2},{1,3},{2,4},{3,5},{4,6},{5,7},{6,0},{7,1},{8,10},{9,11},{10,... | collective-permute-start | bytes 688136 | tf_op jit(solution)/shard_map/ppermute | solution.py:43
  97.3 16.1 %collective-permute-start.21 = (bf16[128,896]{1,0:T(8,128)(2,1)S(1)}, bf16[128,896]{1,0:T(8,128)(2,1)S(1)}, u32[]{:S(2)}, u32[]{:S(2)}) collective-permute-start(bf16[128,896]{1,0:T(8,128)(2,1)S(1)} %get-tuple-element.39.refs_1_), channel_id=1, source_target_pairs={{0,4},{1,5},{2,6},{3,7},{4,0},{5,1},{6,2},{7,3},{8,12},{9,13},{10,... | collective-permute-start | bytes 688136 | tf_op jit(solution)/shard_map/ppermute | solution.py:43
  98.0 18.5 %collective-permute-start.20 = (bf16[128,896]{1,0:T(8,128)(2,1)S(1)}, bf16[128,896]{1,0:T(8,128)(2,1)S(1)}, u32[]{:S(2)}, u32[]{:S(2)}) collective-permute-start(bf16[128,896]{1,0:T(8,128)(2,1)S(1)} %get-tuple-element.39.refs_1_), channel_id=1, source_target_pairs={{0,6},{1,7},{2,0},{3,1},{4,2},{5,3},{6,4},{7,5},{8,14},{9,15},{10,... | collective-permute-start | bytes 688136 | tf_op jit(solution)/shard_map/ppermute | solution.py:43
  100.2 16.3 %collective-permute-start.23 = (bf16[128,896]{1,0:T(8,128)(2,1)S(1)}, bf16[128,896]{1,0:T(8,128)(2,1)S(1)}, u32[]{:S(2)}, u32[]{:S(2)}) collective-permute-start(bf16[128,896]{1,0:T(8,128)(2,1)S(1)} %get-tuple-element.39.refs_1_), channel_id=1, source_target_pairs={{0,1},{1,0},{2,3},{3,2},{4,5},{5,4},{6,7},{7,6},{8,9},{9,8},{10,11... | collective-permute-start | bytes 688136 | tf_op jit(solution)/shard_map/ppermute | solution.py:47
  105.3 11.2 %collective-permute-start.26 = (bf16[128,896]{1,0:T(8,128)(2,1)S(1)}, bf16[128,896]{1,0:T(8,128)(2,1)S(1)}, u32[]{:S(2)}, u32[]{:S(2)}) collective-permute-start(bf16[128,896]{1,0:T(8,128)(2,1)S(1)} %collective-permute-done.22.refs_4_), channel_id=1, source_target_pairs={{0,1},{1,0},{2,3},{3,2},{4,5},{5,4},{6,7},{7,6},{8,9},{9,8},{10,11... | collective-permute-start | bytes 688136 | tf_op jit(solution)/shard_map/ppermute | solution.py:47
  124.2 40.2 %all-to-all-start = ((bf16[32,32,1024]{2,1,0:T(8,128)(2,1)}), bf16[32,32,1024]{2,1,0:T(8,128)(2,1)S(1)}, u32[]{:S(2)}, u32[]{:S(2)}) async-start(bf16[32,32,1024]{2,1,0:T(8,128)(2,1)} %bitcast.6), calls=%async_computation | async-start | bytes 4194304 | tf_op jit(solution)/shard_map/all_to_all | solution.py:305
  (17 other events, 218.9 us)
where the time goes:
time: 167 us; the launch traced here: 166 us
  waiting for transfers between devices  79.8 us (48%)
  starting transfers between devices  53 us (32%)
  Pallas kernels  27.8 us (17%)
  local copies, waits for them, and re-layouts  4.4 us (3%)
    ppermute x10, waiting for transfers between devices, shift_zh(): lax.ppermute(value, 'wid', [(w, (w + 2 * step) % 8) for w in range(8)])  39.7 us
    pallas_call x9, Pallas kernels, run(): pl.pallas_call(body, out_shape=[(pltpu.HBM if o[2:] else jax.ShapeDtypeSt...  27.8 us
    ppermute x10, starting transfers between devices, shift_zh(): lax.ppermute(value, 'wid', [(w, (w + 2 * step) % 8) for w in range(8)])  23.6 us
    all_to_all x1, waiting for transfers between devices, per_device(): lax.all_to_all(partial, 'hid', split_axis=0, concat_axis=0, tiled=True)  21.2 us
    all_to_all x1, starting transfers between devices, per_device(): lax.all_to_all(partial, 'hid', split_axis=0, concat_axis=0, tiled=True)  7.62 us
    ppermute x2, starting transfers between devices, swap_y(): return lax.ppermute(value, 'hid', [(h, h ^ 2 * bit) for h in range(32)])  7.12 us
    ppermute x3, waiting for transfers between devices, shift_y(): lax.ppermute(value, 'hid', [(h, h // 8 * 8 + (h % 8 + 2 * step) % 8) for...  5.41 us
    ppermute x6, waiting for transfers between devices, swap_core(): return lax.ppermute(value, 'wid', [(w, w ^ 1) for w in range(8)])  5.24 us
  transfers between devices with their start and end apart: 29, of which 17 were waited for; matrix products, arithmetic and copies ran while one was open for 0% of the time, Pallas kernels for 8%

commit v1 on v0

--- a/solution.py
+++ b/solution.py
@@ -138,30 +138,30 @@
     rows_out[128:] = far[...]
 
 
-def pair_sum_kernel(pos, keep, got, *refs):
-    acts = refs[:5]
-    own, one, two, three, acts_out, sems = refs[5:]
-    copies = []
-    for i, (block, row) in enumerate(zip(acts, (0, 256, 768, 512, 640))):
-        place = acts_out.at[pl.ds(row, block.shape[0])]
-        copies.append(pltpu.make_async_copy(block, place, sems.at[i]))
-    start_all(copies)
+def acts_kernel(pos, here, below, above, far_gate, far_up, out):
+    row = 0
+    for block in (here, below, far_gate, far_up, above):
+        rows = block.shape[0]
+        out[row : row + rows] = block[...]
+        row += rows
+
+
+def pair_sum_kernel(pos, keep, got, own, one, two, three):
     own[...] = keep[:128] + got[:128]
     for k, out in enumerate((one, two, three)):
         rows = slice(128 * (k + 1), 128 * (k + 2))
         out[...] = (keep[rows] + got[rows]).astype(BF)
-    wait_all(copies)
-
-
-def ring_sum_kernel(pos, own, one, two, three, near, far, out, rows_out):
+
+
+def ring_sum_kernel(pos, own, one, two, three, out):
+    total = own[...] + one[...].astype(F32) + two[...].astype(F32) + three[...].astype(F32)
+    out[...] = total.astype(BF)
+
+
+def down_kernel(pos, *refs):
+    blocks, near, far, grads, out, act_out, slope_out, rows_out, hidden = refs[:2], *refs[2:]
     rows_out[:256] = near[...]
     rows_out[256:] = far[...]
-    total = own[...] + one[...].astype(F32) + two[...].astype(F32) + three[...].astype(F32)
-    out[...] = total.astype(BF)
-
-
-def down_kernel(pos, *refs):
-    blocks, (grads, out, act_out, slope_out, hidden) = refs[:2], refs[2:]
     for i in range(8):
         rows = slice(i * 128, (i + 1) * 128)
         start = 256 * (i % 4)
@@ -271,24 +271,19 @@
         after=2,
     )(pos, block, *[shift_y(block, k) for k in (1, 2, 3)], w_down, near, far, *acts[3:])
     far = swap_y(near, 2)
-    own, one, two, three, acts = call(
-        pair_sum_kernel,
-        [((128, FB), F32)] + [((128, FB), BF)] * 3 + [((T, FB), BF)],
-        LONG,
-        [pltpu.SemaphoreType.DMA((5,))],
-        whole=5,
-    )(pos, keep, swap_core(send), *acts)
+    (acts,) = call(acts_kernel, [((T, FB), BF)], SHORT, after=1)(pos, *acts, near)
+    own, one, two, three = call(
+        pair_sum_kernel, [((128, FB), F32)] + [((128, FB), BF)] * 3, LONG
+    )(pos, keep, swap_core(send))
     got = [shift_zh(one, 1), shift_zh(two, 2), shift_zh(three, 3)]
-    grad_down, act, slope = call(
+    grad_down, act, slope, near = call(
         down_kernel,
-        [((FB, DB), BF), ((T, FB), F32), ((T, FB), F32)],
+        [((FB, DB), BF), ((T, FB), F32), ((T, FB), F32), ((512, DB), BF)],
         (MM, 16 * MB),
         [pltpu.VMEM((T, FB), BF)],
-    )(pos, acts, swap_core(acts), all_grads)
-    hg, near = call(
-        ring_sum_kernel, [((128, FB), BF), ((512, DB), BF)], LONG, after=1
-    )(pos, own, *got, near, far, act)
+    )(pos, acts, swap_core(acts), near, far, all_grads)
     far = swap_x(near, 2)
+    (hg,) = call(ring_sum_kernel, [((128, FB), BF)], LONG, after=1)(pos, own, *got, act)
     hgs = spread_core(gather_zh(hg))
     partial, gate_grad, up_grad = call(
         input_grad_kernel,

time: 167 us -> 163 us (0.976)
  starting transfers between devices: 53 us -> 50.6 us
    ppermute x6, waiting for transfers between devices: 5.24 us -> 1.47 us  [swap_core(): return lax.ppermute(value, 'wid', [(w, w ^ 1) for w in range(8)])]
    all_to_all x1, starting transfers between devices: 7.62 us -> 4.02 us  [per_device(): lax.all_to_all(partial, 'hid', split_axis=0, concat_axis=0, tiled=True)]
    ppermute x2, waiting for transfers between devices: 2.72 us -> 5.84 us  [swap_y(): return lax.ppermute(value, 'hid', [(h, h ^ 2 * bit) for h in range(32)])]
    ppermute x10, waiting for transfers between devices: 39.7 us -> 37.9 us  [shift_zh(): lax.ppermute(value, 'wid', [(w, (w + 2 * step) % 8) for w in range(8)])]
    pallas_call x9 -> x10, Pallas kernels: 27.8 us -> 27.2 us  [run(): pl.pallas_call(body, out_shape=[(pltpu.HBM if o[2:] else jax.ShapeDtypeSt...]
    unnamed x25 -> x15, local copies, waits for them, and re-layouts: 4.26 us -> 4.24 us
  transfers between devices with their start and end apart: 29 -> 29, of which waited for: 17 -> 16; matrix products, arithmetic and copies ran while one was open for 0% -> 0% of each run, Pallas kernels for 8% -> 9%
where the time goes in v1:
time: 163 us; the launch traced here: 162 us
  waiting for transfers between devices  78.5 us (48%)
  starting transfers between devices  50.6 us (31%)
  Pallas kernels  27.2 us (17%)
  local copies, waits for them, and re-layouts  4.37 us (3%)
    ppermute x10, waiting for transfers between devices, shift_zh(): lax.ppermute(value, 'wid', [(w, (w + 2 * step) % 8) for w in range(8)])  37.9 us
    pallas_call x10, Pallas kernels, run(): pl.pallas_call(body, out_shape=[(pltpu.HBM if o[2:] else jax.ShapeDtypeSt...  27.2 us
    ppermute x10, starting transfers between devices, shift_zh(): lax.ppermute(value, 'wid', [(w, (w + 2 * step) % 8) for w in range(8)])  23.4 us
    all_to_all x1, waiting for transfers between devices, per_device(): lax.all_to_all(partial, 'hid', split_axis=0, concat_axis=0, tiled=True)  22.4 us
    ppermute x2, starting transfers between devices, swap_y(): return lax.ppermute(value, 'hid', [(h, h ^ 2 * bit) for h in range(32)])  7.38 us
    ppermute x2, waiting for transfers between devices, swap_y(): return lax.ppermute(value, 'hid', [(h, h ^ 2 * bit) for h in range(32)])  5.84 us
    ppermute x3, waiting for transfers between devices, shift_y(): lax.ppermute(value, 'hid', [(h, h // 8 * 8 + (h % 8 + 2 * step) % 8) for...  5.41 us
    ppermute x3, starting transfers between devices, shift_y(): lax.ppermute(value, 'hid', [(h, h // 8 * 8 + (h % 8 + 2 * step) % 8) for...  4.69 us
  transfers between devices with their start and end apart: 29, of which 16 were waited for; matrix products, arithmetic and copies ran while one was open for 0% of the time, Pallas kernels for 9%

profile of v1, /device:TPU:64, one launch (start us, length us, event | category | flops | bytes accessed | tf_op | source)
XLA Modules:
  0.0 161.5 jit_solution(1978066694405519498)
XLA Ops:
  2.8 2.6 %collective-permute-done.1.refs_2_ = bf16[32,1024]{1,0:T(8,128)(2,1)S(1)} collective-permute-done((bf16[32,1024]{1,0:T(8,128)(2,1)}, bf16[32,1024]{1,0:T(8,128)(2,1)S(1)}, u32[]{:S(2)}, u32[]{:S(2)}) %collective-permute-start.1) | collective-permute-done | bytes 65568 | tf_op jit(solution)/shard_map/ppermute | solution.py:39
  9.2 2.7 %collective-permute-start.4 = (bf16[64,1024]{1,0:T(8,128)(2,1)S(1)}, bf16[64,1024]{1,0:T(8,128)(2,1)S(1)}, u32[]{:S(2)}, u32[]{:S(2)}) collective-permute-start(bf16[64,1024]{1,0:T(8,128)(2,1)S(1)} %get-tuple-element.24.refs_1_), channel_id=1, source_target_pairs={{0,192},{8,200},{16,208},{24,216},{32,224},{40,232},{48,240},{56,2... | collective-permute-start | bytes 393224 | tf_op jit(solution)/shard_map/ppermute | solution.py:21
  16.3 4.1 %collective-permute-start.10 = (bf16[256,896]{1,0:T(8,128)(2,1)S(1)}, bf16[256,896]{1,0:T(8,128)(2,1)S(1)}, u32[]{:S(2)}, u32[]{:S(2)}) collective-permute-start(bf16[256,896]{1,0:T(8,128)(2,1)S(1)} %get-tuple-element.26.refs_1_), channel_id=1, source_target_pairs={{0,2},{1,3},{2,4},{3,5},{4,6},{5,7},{6,0},{7,1},{8,10},{9,11},{10,... | collective-permute-start | bytes 1376264 | tf_op jit(solution)/shard_map/ppermute | solution.py:43
  21.0 3.1 %collective-permute-start.7 = (bf16[256,1024]{1,0:T(8,128)(2,1)S(1)}, bf16[256,1024]{1,0:T(8,128)(2,1)S(1)}, u32[]{:S(2)}, u32[]{:S(2)}) collective-permute-start(bf16[256,1024]{1,0:T(8,128)(2,1)S(1)} %shard_map.103.refs_1_), channel_id=1, source_target_pairs={{0,48},{8,56},{16,0},{24,8},{32,16},{40,24},{48,32},{56,40},{64,11... | collective-permute-start | bytes 1572872 | tf_op jit(solution)/shard_map/ppermute | solution.py:25
  25.7 6.5 %collective-permute-done.12.refs_2_ = bf16[256,896]{1,0:T(8,128)(2,1)S(1)} collective-permute-done((bf16[256,896]{1,0:T(8,128)(2,1)S(1)}, bf16[256,896]{1,0:T(8,128)(2,1)S(1)}, u32[]{:S(2)}, u32[]{:S(2)}) %collective-permute-start.12) | collective-permute-done | bytes 458784 | tf_op jit(solution)/shard_map/ppermute | solution.py:43
  33.8 8.0 %collective-permute-start.13 = (bf16[128,896]{1,0:T(8,128)(2,1)S(1)}, bf16[128,896]{1,0:T(8,128)(2,1)S(1)}, u32[]{:S(2)}, u32[]{:S(2)}) collective-permute-start(bf16[128,896]{1,0:T(8,128)(2,1)S(1)} %slice.9), channel_id=1, source_target_pairs={{0,6},{1,7},{2,0},{3,1},{4,2},{5,3},{6,4},{7,5},{8,14},{9,15},{10,... | collective-permute-start | bytes 688136 | tf_op jit(solution)/shard_map/ppermute | solution.py:43
  43.6 3.7 %collective-permute-done.5.refs_2_ = bf16[256,1024]{1,0:T(8,128)(2,1)S(1)} collective-permute-done((bf16[256,1024]{1,0:T(8,128)(2,1)S(1)}, bf16[256,1024]{1,0:T(8,128)(2,1)S(1)}, u32[]{:S(2)}, u32[]{:S(2)}) %collective-permute-start.5) | collective-permute-done | bytes 524320 | tf_op jit(solution)/shard_map/ppermute | solution.py:25
  49.5 3.0 %shard_map.104 = (bf16[1024,1024]{1,0:T(8,128)(2,1)S(1)}, f32[512,896]{1,0:T(8,128)S(1)}, f32[512,896]{1,0:T(8,128)S(1)}, bf16[256,1024]{1,0:T(8,128)(2,1)S(1)}) custom-call(s32[5]{0:T(128)S(1)} %stack.23.refs_0_, bf16[256,1024]{1,0:T(8,128)(2,1)S(1)} %shard_map.103.refs_1_, bf16[256,1024]{1,0:T(8,128)(2,1)S(1)} %collective-permute-done.5.refs_2_, ...), custom_call_target="tpu_custom_call" | custom-call | flops 22548578304 | bytes 83886080 | tf_op jit(solution)/shard_map/pallas_call | solution.py:83
  52.6 5.8 %collective-permute-start.19 = (bf16[256,1024]{1,0:T(8,128)(2,1)S(1)}, bf16[256,1024]{1,0:T(8,128)(2,1)S(1)}, u32[]{:S(2)}, u32[]{:S(2)}) collective-permute-start(bf16[256,1024]{1,0:T(8,128)(2,1)S(1)} %get-tuple-element.33.refs_6_.refs_3_), channel_id=1, source_target_pairs={{0,32},{8,40},{16,48},{24,56},{32,0},{40,8},{48,16},{56,24},{64,96... | collective-permute-start | bytes 1572872 | tf_op jit(solution)/shard_map/ppermute | solution.py:35
  61.0 3.8 %collective-permute-start.16 = (bf16[128,896]{1,0:T(8,128)(2,1)S(1)}, bf16[128,896]{1,0:T(8,128)(2,1)S(1)}, u32[]{:S(2)}, u32[]{:S(2)}) collective-permute-start(bf16[128,896]{1,0:T(8,128)(2,1)S(1)} %get-tuple-element.31), channel_id=1, source_target_pairs={{0,4},{1,5},{2,6},{3,7},{4,0},{5,1},{6,2},{7,3},{8,12},{9,13},{10,... | collective-permute-start | bytes 688136 | tf_op jit(solution)/shard_map/ppermute | solution.py:43
  64.9 5.8 %collective-permute-done.19.refs_4_ = bf16[256,1024]{1,0:T(8,128)(2,1)S(1)} collective-permute-done((bf16[256,1024]{1,0:T(8,128)(2,1)S(1)}, bf16[256,1024]{1,0:T(8,128)(2,1)S(1)}, u32[]{:S(2)}, u32[]{:S(2)}) %collective-permute-start.19) | collective-permute-done | bytes 524320 | tf_op jit(solution)/shard_map/ppermute | solution.py:35
  70.7 4.9 %shard_map.107 = (bf16[896,1024]{1,0:T(8,128)(2,1)}, f32[1024,896]{1,0:T(8,128)S(1)}, f32[1024,896]{1,0:T(8,128)S(1)}, bf16[512,1024]{1,0:T(8,128)(2,1)S(1)}) custom-call(s32[5]{0:T(128)S(1)} %stack.23.refs_0_, bf16[1024,896]{1,0:T(8,128)(2,1)S(1)} %shard_map.106.refs_1_, bf16[1024,896]{1,0:T(8,128)(2,1)S(1)} %collective-permute-done.18.refs_2_, ...), custom_call_target="tpu_custom_call" | custom-call | flops 1879048192 | bytes 16777216 | tf_op jit(solution)/shard_map/pallas_call | solution.py:83
  75.6 3.0 %collective-permute-start.27 = (bf16[512,1024]{1,0:T(8,128)(2,1)S(1)}, bf16[512,1024]{1,0:T(8,128)(2,1)S(1)}, u32[]{:S(2)}, u32[]{:S(2)}) collective-permute-start(bf16[512,1024]{1,0:T(8,128)(2,1)S(1)} %get-tuple-element.37.refs_1_), channel_id=1, source_target_pairs={{0,128},{8,136},{16,144},{24,152},{32,160},{40,168},{48,176},{56,1... | collective-permute-start | bytes 3145736 | tf_op jit(solution)/shard_map/ppermute | solution.py:31
  78.6 7.0 %collective-permute-done.16.refs_3_ = bf16[128,896]{1,0:T(8,128)(2,1)S(1)} collective-permute-done((bf16[128,896]{1,0:T(8,128)(2,1)S(1)}, bf16[128,896]{1,0:T(8,128)(2,1)S(1)}, u32[]{:S(2)}, u32[]{:S(2)}) %collective-permute-start.16) | collective-permute-done | bytes 229408 | tf_op jit(solution)/shard_map/ppermute | solution.py:43
  85.6 2.1 %collective-permute-done.17.refs_4_ = bf16[128,896]{1,0:T(8,128)(2,1)S(1)} collective-permute-done((bf16[128,896]{1,0:T(8,128)(2,1)S(1)}, bf16[128,896]{1,0:T(8,128)(2,1)S(1)}, u32[]{:S(2)}, u32[]{:S(2)}) %collective-permute-start.17) | collective-permute-done | bytes 229408 | tf_op jit(solution)/shard_map/ppermute | solution.py:43
  88.4 2.1 %collective-permute-start.22 = (bf16[128,896]{1,0:T(8,128)(2,1)S(1)}, bf16[128,896]{1,0:T(8,128)(2,1)S(1)}, u32[]{:S(2)}, u32[]{:S(2)}) collective-permute-start(bf16[128,896]{1,0:T(8,128)(2,1)S(1)} %shard_map.108.refs_1_), channel_id=1, source_target_pairs={{0,2},{1,3},{2,4},{3,5},{4,6},{5,7},{6,0},{7,1},{8,10},{9,11},{10,... | collective-permute-start | bytes 688136 | tf_op jit(solution)/shard_map/ppermute | solution.py:43
  90.4 2.3 %collective-permute-start.21 = (bf16[128,896]{1,0:T(8,128)(2,1)S(1)}, bf16[128,896]{1,0:T(8,128)(2,1)S(1)}, u32[]{:S(2)}, u32[]{:S(2)}) collective-permute-start(bf16[128,896]{1,0:T(8,128)(2,1)S(1)} %shard_map.108.refs_1_), channel_id=1, source_target_pairs={{0,4},{1,5},{2,6},{3,7},{4,0},{5,1},{6,2},{7,3},{8,12},{9,13},{10,... | collective-permute-start | bytes 688136 | tf_op jit(solution)/shard_map/ppermute | solution.py:43
  94.4 5.9 %collective-permute-done.22.refs_4_ = bf16[128,896]{1,0:T(8,128)(2,1)S(1)} collective-permute-done((bf16[128,896]{1,0:T(8,128)(2,1)S(1)}, bf16[128,896]{1,0:T(8,128)(2,1)S(1)}, u32[]{:S(2)}, u32[]{:S(2)}) %collective-permute-start.22) | collective-permute-done | bytes 229408 | tf_op jit(solution)/shard_map/ppermute | solution.py:43
  100.2 7.0 %collective-permute-done.21.refs_3_ = bf16[128,896]{1,0:T(8,128)(2,1)S(1)} collective-permute-done((bf16[128,896]{1,0:T(8,128)(2,1)S(1)}, bf16[128,896]{1,0:T(8,128)(2,1)S(1)}, u32[]{:S(2)}, u32[]{:S(2)}) %collective-permute-start.21) | collective-permute-done | bytes 229408 | tf_op jit(solution)/shard_map/ppermute | solution.py:43
  107.2 7.3 %collective-permute-done.20.refs_2_ = bf16[128,896]{1,0:T(8,128)(2,1)S(1)} collective-permute-done((bf16[128,896]{1,0:T(8,128)(2,1)S(1)}, bf16[128,896]{1,0:T(8,128)(2,1)S(1)}, u32[]{:S(2)}, u32[]{:S(2)}) %collective-permute-start.20) | collective-permute-done | bytes 229408 | tf_op jit(solution)/shard_map/ppermute | solution.py:43
  116.0 6.2 %shard_map.109 = (bf16[1024,1024]{1,0:T(8,128)(2,1)}, bf16[1024,896]{1,0:T(8,128)(2,1)}, bf16[1024,896]{1,0:T(8,128)(2,1)}) custom-call(s32[5]{0:T(128)S(1)} %stack.23.refs_0_, bf16[128,896]{1,0:T(8,128)(2,1)S(1)} %shard_map.108.refs_1_, bf16[128,896]{1,0:T(8,128)(2,1)S(1)} %collective-permute-done.20.refs_2_, ...), custom_call_target="tpu_custom_call" | custom-call | flops 3758096384 | bytes 15728640 | tf_op jit(solution)/shard_map/pallas_call | solution.py:83
  122.3 4.0 %all-to-all-start = ((bf16[32,32,1024]{2,1,0:T(8,128)(2,1)}), bf16[32,32,1024]{2,1,0:T(8,128)(2,1)S(1)}, u32[]{:S(2)}, u32[]{:S(2)}) async-start(bf16[32,32,1024]{2,1,0:T(8,128)(2,1)} %bitcast.6), calls=%async_computation | async-start | bytes 4194304 | tf_op jit(solution)/shard_map/all_to_all | solution.py:300
  130.6 7.1 %shard_map.111 = (bf16[1024,896]{1,0:T(8,128)(2,1)}, bf16[1024,896]{1,0:T(8,128)(2,1)}) custom-call(s32[5]{0:T(128)S(1)} %stack.23.refs_0_, bf16[512,1024]{1,0:T(8,128)(2,1)S(1)} %get-tuple-element.37.refs_1_, bf16[512,1024]{1,0:T(8,128)(2,1)S(1)} %copy-done.4, bf16[1024,896]{1,0:T(8,128)(2,1)S(1)} %copy-done.5, bf16[1024,896]{1,0:T(8,128)(2,1)S(1)} %copy-done.6), custom_call_target="tpu_custom_call" | custom-call | flops 3758096384 | bytes 10485760 | tf_op jit(solution)/shard_map/pallas_call | solution.py:83
  137.7 22.4 %all-to-all-done.refs_1_ = bf16[32,32,1024]{2,1,0:T(8,128)(2,1)S(1)} async-done(((bf16[32,32,1024]{2,1,0:T(8,128)(2,1)}), bf16[32,32,1024]{2,1,0:T(8,128)(2,1)S(1)}, u32[]{:S(2)}, u32[]{:S(2)}) %all-to-all-start) | async-done | bytes 2097184 | tf_op jit(solution)/shard_map/all_to_all | solution.py:300
  (63 shorter events, 30.2 us)
Async XLA Ops:
  9.0 23.3 %collective-permute-start.12 = (bf16[256,896]{1,0:T(8,128)(2,1)S(1)}, bf16[256,896]{1,0:T(8,128)(2,1)S(1)}, u32[]{:S(2)}, u32[]{:S(2)}) collective-permute-start(bf16[256,896]{1,0:T(8,128)(2,1)S(1)} %get-tuple-element.26.refs_1_), channel_id=1, source_target_pairs={{0,6},{1,7},{2,0},{3,1},{4,2},{5,3},{6,4},{7,5},{8,14},{9,15},{10,... | collective-permute-start | bytes 1376264 | tf_op jit(solution)/shard_map/ppermute | solution.py:43
  11.9 8.5 %collective-permute-start.3 = (bf16[64,1024]{1,0:T(8,128)(2,1)S(1)}, bf16[64,1024]{1,0:T(8,128)(2,1)S(1)}, u32[]{:S(2)}, u32[]{:S(2)}) collective-permute-start(bf16[64,1024]{1,0:T(8,128)(2,1)S(1)} %get-tuple-element.24.refs_1_), channel_id=1, source_target_pairs={{0,128},{8,136},{16,144},{24,152},{32,160},{40,168},{48,176},{56,1... | collective-permute-start | bytes 393224 | tf_op jit(solution)/shard_map/ppermute | solution.py:21
  12.7 7.7 %collective-permute-start.2 = (bf16[64,1024]{1,0:T(8,128)(2,1)S(1)}, bf16[64,1024]{1,0:T(8,128)(2,1)S(1)}, u32[]{:S(2)}, u32[]{:S(2)}) collective-permute-start(bf16[64,1024]{1,0:T(8,128)(2,1)S(1)} %get-tuple-element.24.refs_1_), channel_id=1, source_target_pairs={{0,64},{8,72},{16,80},{24,88},{32,96},{40,104},{48,112},{56,120},{... | collective-permute-start | bytes 393224 | tf_op jit(solution)/shard_map/ppermute | solution.py:21
  13.6 11.2 %collective-permute-start.8 = (bf16[64,1024]{1,0:T(8,128)(2,1)S(1)}, bf16[64,1024]{1,0:T(8,128)(2,1)S(1)}, u32[]{:S(2)}, u32[]{:S(2)}) collective-permute-start(bf16[64,1024]{1,0:T(8,128)(2,1)S(1)} %get-tuple-element.25), channel_id=1, source_target_pairs={{0,16},{8,24},{16,0},{24,8},{32,48},{40,56},{48,32},{56,40},{64,80... | collective-permute-start | bytes 393224 | tf_op jit(solution)/shard_map/ppermute | solution.py:35
  16.3 17.4 %collective-permute-start.10 = (bf16[256,896]{1,0:T(8,128)(2,1)S(1)}, bf16[256,896]{1,0:T(8,128)(2,1)S(1)}, u32[]{:S(2)}, u32[]{:S(2)}) collective-permute-start(bf16[256,896]{1,0:T(8,128)(2,1)S(1)} %get-tuple-element.26.refs_1_), channel_id=1, source_target_pairs={{0,2},{1,3},{2,4},{3,5},{4,6},{5,7},{6,0},{7,1},{8,10},{9,11},{10,... | collective-permute-start | bytes 1376264 | tf_op jit(solution)/shard_map/ppermute | solution.py:43
  21.0 22.6 %collective-permute-start.7 = (bf16[256,1024]{1,0:T(8,128)(2,1)S(1)}, bf16[256,1024]{1,0:T(8,128)(2,1)S(1)}, u32[]{:S(2)}, u32[]{:S(2)}) collective-permute-start(bf16[256,1024]{1,0:T(8,128)(2,1)S(1)} %shard_map.103.refs_1_), channel_id=1, source_target_pairs={{0,48},{8,56},{16,0},{24,8},{32,16},{40,24},{48,32},{56,40},{64,11... | collective-permute-start | bytes 1572872 | tf_op jit(solution)/shard_map/ppermute | solution.py:25
  24.1 19.5 %collective-permute-start.6 = (bf16[256,1024]{1,0:T(8,128)(2,1)S(1)}, bf16[256,1024]{1,0:T(8,128)(2,1)S(1)}, u32[]{:S(2)}, u32[]{:S(2)}) collective-permute-start(bf16[256,1024]{1,0:T(8,128)(2,1)S(1)} %shard_map.103.refs_1_), channel_id=1, source_target_pairs={{0,32},{8,40},{16,48},{24,56},{32,0},{40,8},{48,16},{56,24},{64,96... | collective-permute-start | bytes 1572872 | tf_op jit(solution)/shard_map/ppermute | solution.py:25
  24.8 22.5 %collective-permute-start.5 = (bf16[256,1024]{1,0:T(8,128)(2,1)S(1)}, bf16[256,1024]{1,0:T(8,128)(2,1)S(1)}, u32[]{:S(2)}, u32[]{:S(2)}) collective-permute-start(bf16[256,1024]{1,0:T(8,128)(2,1)S(1)} %shard_map.103.refs_1_), channel_id=1, source_target_pairs={{0,16},{8,24},{16,32},{24,40},{32,48},{40,56},{48,0},{56,8},{64,80... | collective-permute-start | bytes 1572872 | tf_op jit(solution)/shard_map/ppermute | solution.py:25
  32.2 9.6 %collective-permute-start.9 = (bf16[128,1024]{1,0:T(8,128)(2,1)S(1)}, bf16[128,1024]{1,0:T(8,128)(2,1)S(1)}, u32[]{:S(2)}, u32[]{:S(2)}) collective-permute-start(bf16[128,1024]{1,0:T(8,128)(2,1)S(1)} %constant_dynamic-update-slice_fusion.refs_6_), channel_id=1, source_target_pairs={{0,64},{8,72},{16,80},{24,88},{32,96},{40,104},{48,112},{56,120},{... | collective-permute-start | bytes 786440 | tf_op jit(solution)/shard_map/ppermute | solution.py:31
  33.8 15.2 %collective-permute-start.13 = (bf16[128,896]{1,0:T(8,128)(2,1)S(1)}, bf16[128,896]{1,0:T(8,128)(2,1)S(1)}, u32[]{:S(2)}, u32[]{:S(2)}) collective-permute-start(bf16[128,896]{1,0:T(8,128)(2,1)S(1)} %slice.9), channel_id=1, source_target_pairs={{0,6},{1,7},{2,0},{3,1},{4,2},{5,3},{6,4},{7,5},{8,14},{9,15},{10,... | collective-permute-start | bytes 688136 | tf_op jit(solution)/shard_map/ppermute | solution.py:43
  41.8 7.7 %collective-permute-start.11 = (bf16[128,896]{1,0:T(8,128)(2,1)S(1)}, bf16[128,896]{1,0:T(8,128)(2,1)S(1)}, u32[]{:S(2)}, u32[]{:S(2)}) collective-permute-start(bf16[128,896]{1,0:T(8,128)(2,1)S(1)} %slice.8), channel_id=1, source_target_pairs={{0,2},{1,3},{2,4},{3,5},{4,6},{5,7},{6,0},{7,1},{8,10},{9,11},{10,... | collective-permute-start | bytes 688136 | tf_op jit(solution)/shard_map/ppermute | solution.py:43
  52.6 18.1 %collective-permute-start.19 = (bf16[256,1024]{1,0:T(8,128)(2,1)S(1)}, bf16[256,1024]{1,0:T(8,128)(2,1)S(1)}, u32[]{:S(2)}, u32[]{:S(2)}) collective-permute-start(bf16[256,1024]{1,0:T(8,128)(2,1)S(1)} %get-tuple-element.33.refs_6_.refs_3_), channel_id=1, source_target_pairs={{0,32},{8,40},{16,48},{24,56},{32,0},{40,8},{48,16},{56,24},{64,96... | collective-permute-start | bytes 1572872 | tf_op jit(solution)/shard_map/ppermute | solution.py:35
  59.1 11.6 %collective-permute-start.18 = (bf16[1024,896]{1,0:T(8,128)(2,1)S(1)}, bf16[1024,896]{1,0:T(8,128)(2,1)S(1)}, u32[]{:S(2)}, u32[]{:S(2)}) collective-permute-start(bf16[1024,896]{1,0:T(8,128)(2,1)S(1)} %shard_map.106.refs_1_), channel_id=1, source_target_pairs={{0,1},{1,0},{2,3},{3,2},{4,5},{5,4},{6,7},{7,6},{8,9},{9,8},{10,11... | collective-permute-start | bytes 5505032 | tf_op jit(solution)/shard_map/ppermute | solution.py:47
  59.9 18.7 %collective-permute-start.15 = (bf16[128,896]{1,0:T(8,128)(2,1)S(1)}, bf16[128,896]{1,0:T(8,128)(2,1)S(1)}, u32[]{:S(2)}, u32[]{:S(2)}) collective-permute-start(bf16[128,896]{1,0:T(8,128)(2,1)S(1)} %get-tuple-element.30), channel_id=1, source_target_pairs={{0,2},{1,3},{2,4},{3,5},{4,6},{5,7},{6,0},{7,1},{8,10},{9,11},{10,... | collective-permute-start | bytes 688136 | tf_op jit(solution)/shard_map/ppermute | solution.py:43
  61.0 24.6 %collective-permute-start.16 = (bf16[128,896]{1,0:T(8,128)(2,1)S(1)}, bf16[128,896]{1,0:T(8,128)(2,1)S(1)}, u32[]{:S(2)}, u32[]{:S(2)}) collective-permute-start(bf16[128,896]{1,0:T(8,128)(2,1)S(1)} %get-tuple-element.31), channel_id=1, source_target_pairs={{0,4},{1,5},{2,6},{3,7},{4,0},{5,1},{6,2},{7,3},{8,12},{9,13},{10,... | collective-permute-start | bytes 688136 | tf_op jit(solution)/shard_map/ppermute | solution.py:43
  64.9 22.8 %collective-permute-start.17 = (bf16[128,896]{1,0:T(8,128)(2,1)S(1)}, bf16[128,896]{1,0:T(8,128)(2,1)S(1)}, u32[]{:S(2)}, u32[]{:S(2)}) collective-permute-start(bf16[128,896]{1,0:T(8,128)(2,1)S(1)} %get-tuple-element.32), channel_id=1, source_target_pairs={{0,6},{1,7},{2,0},{3,1},{4,2},{5,3},{6,4},{7,5},{8,14},{9,15},{10,... | collective-permute-start | bytes 688136 | tf_op jit(solution)/shard_map/ppermute | solution.py:43
  75.6 40.4 %collective-permute-start.27 = (bf16[512,1024]{1,0:T(8,128)(2,1)S(1)}, bf16[512,1024]{1,0:T(8,128)(2,1)S(1)}, u32[]{:S(2)}, u32[]{:S(2)}) collective-permute-start(bf16[512,1024]{1,0:T(8,128)(2,1)S(1)} %get-tuple-element.37.refs_1_), channel_id=1, source_target_pairs={{0,128},{8,136},{16,144},{24,152},{32,160},{40,168},{48,176},{56,1... | collective-permute-start | bytes 3145736 | tf_op jit(solution)/shard_map/ppermute | solution.py:31
  88.4 11.9 %collective-permute-start.22 = (bf16[128,896]{1,0:T(8,128)(2,1)S(1)}, bf16[128,896]{1,0:T(8,128)(2,1)S(1)}, u32[]{:S(2)}, u32[]{:S(2)}) collective-permute-start(bf16[128,896]{1,0:T(8,128)(2,1)S(1)} %shard_map.108.refs_1_), channel_id=1, source_target_pairs={{0,2},{1,3},{2,4},{3,5},{4,6},{5,7},{6,0},{7,1},{8,10},{9,11},{10,... | collective-permute-start | bytes 688136 | tf_op jit(solution)/shard_map/ppermute | solution.py:43
  90.4 16.8 %collective-permute-start.21 = (bf16[128,896]{1,0:T(8,128)(2,1)S(1)}, bf16[128,896]{1,0:T(8,128)(2,1)S(1)}, u32[]{:S(2)}, u32[]{:S(2)}) collective-permute-start(bf16[128,896]{1,0:T(8,128)(2,1)S(1)} %shard_map.108.refs_1_), channel_id=1, source_target_pairs={{0,4},{1,5},{2,6},{3,7},{4,0},{5,1},{6,2},{7,3},{8,12},{9,13},{10,... | collective-permute-start | bytes 688136 | tf_op jit(solution)/shard_map/ppermute | solution.py:43
  92.7 21.8 %collective-permute-start.20 = (bf16[128,896]{1,0:T(8,128)(2,1)S(1)}, bf16[128,896]{1,0:T(8,128)(2,1)S(1)}, u32[]{:S(2)}, u32[]{:S(2)}) collective-permute-start(bf16[128,896]{1,0:T(8,128)(2,1)S(1)} %shard_map.108.refs_1_), channel_id=1, source_target_pairs={{0,6},{1,7},{2,0},{3,1},{4,2},{5,3},{6,4},{7,5},{8,14},{9,15},{10,... | collective-permute-start | bytes 688136 | tf_op jit(solution)/shard_map/ppermute | solution.py:43
  94.4 20.2 %collective-permute-start.23 = (bf16[128,896]{1,0:T(8,128)(2,1)S(1)}, bf16[128,896]{1,0:T(8,128)(2,1)S(1)}, u32[]{:S(2)}, u32[]{:S(2)}) collective-permute-start(bf16[128,896]{1,0:T(8,128)(2,1)S(1)} %shard_map.108.refs_1_), channel_id=1, source_target_pairs={{0,1},{1,0},{2,3},{3,2},{4,5},{5,4},{6,7},{7,6},{8,9},{9,8},{10,11... | collective-permute-start | bytes 688136 | tf_op jit(solution)/shard_map/ppermute | solution.py:47
  100.2 14.3 %collective-permute-start.26 = (bf16[128,896]{1,0:T(8,128)(2,1)S(1)}, bf16[128,896]{1,0:T(8,128)(2,1)S(1)}, u32[]{:S(2)}, u32[]{:S(2)}) collective-permute-start(bf16[128,896]{1,0:T(8,128)(2,1)S(1)} %collective-permute-done.22.refs_4_), channel_id=1, source_target_pairs={{0,1},{1,0},{2,3},{3,2},{4,5},{5,4},{6,7},{7,6},{8,9},{9,8},{10,11... | collective-permute-start | bytes 688136 | tf_op jit(solution)/shard_map/ppermute | solution.py:47
  107.2 7.3 %collective-permute-start.25 = (bf16[128,896]{1,0:T(8,128)(2,1)S(1)}, bf16[128,896]{1,0:T(8,128)(2,1)S(1)}, u32[]{:S(2)}, u32[]{:S(2)}) collective-permute-start(bf16[128,896]{1,0:T(8,128)(2,1)S(1)} %collective-permute-done.21.refs_3_), channel_id=1, source_target_pairs={{0,1},{1,0},{2,3},{3,2},{4,5},{5,4},{6,7},{7,6},{8,9},{9,8},{10,11... | collective-permute-start | bytes 688136 | tf_op jit(solution)/shard_map/ppermute | solution.py:47
  122.3 37.8 %all-to-all-start = ((bf16[32,32,1024]{2,1,0:T(8,128)(2,1)}), bf16[32,32,1024]{2,1,0:T(8,128)(2,1)S(1)}, u32[]{:S(2)}, u32[]{:S(2)}) async-start(bf16[32,32,1024]{2,1,0:T(8,128)(2,1)} %bitcast.6), calls=%async_computation | async-start | bytes 4194304 | tf_op jit(solution)/shard_map/all_to_all | solution.py:300
  (12 other events, 140.5 us)

commit v2 on v1

--- a/solution.py
+++ b/solution.py
@@ -126,7 +126,7 @@
 
 
 def hidden_grad_kernel(pos, *refs):
-    pieces, (w_down, near, far, grads, keep, send, rows_out) = refs[:4], refs[4:]
+    pieces, w_down, rows, (grads, keep, send, rows_out) = refs[:4], refs[4], refs[5:9], refs[9:]
     for j, piece in enumerate(pieces):
         to_local(pos, piece, grads, lambda k, j=j: ((pos[0] - k) & 3, (pos[1] - j) & 3))
     for start, width in COL_TILES:
@@ -134,8 +134,8 @@
         part = dot_nt(grads[...], w_down[cols, :])
         keep[:, cols] = part[:512]
         send[:, cols] = part[512:]
-    rows_out[:128] = near[...]
-    rows_out[128:] = far[...]
+    for i, part in enumerate(rows):
+        rows_out[i * 64 : (i + 1) * 64] = part[...]
 
 
 def acts_kernel(pos, here, below, above, far_gate, far_up, out):
@@ -262,14 +262,14 @@
     (block,) = call(rows_kernel, [((256, DB), BF)], (0, MB))(
         pos, block, *[shift_x(block, k) for k in (1, 2, 3)]
     )
-    near = jnp.concatenate([near, swap_y(near, 1)])
-    far = swap_x(near, 1)
+    near = [near, swap_y(near, 1)]
+    near += [swap_x(part, 1) for part in near]
     all_grads, keep, send, near = call(
         hidden_grad_kernel,
         [((T, DB), BF), ((512, FB), F32), ((512, FB), F32), ((256, DB), BF)],
         LONG,
         after=2,
-    )(pos, block, *[shift_y(block, k) for k in (1, 2, 3)], w_down, near, far, *acts[3:])
+    )(pos, block, *[shift_y(block, k) for k in (1, 2, 3)], w_down, *near, *acts[3:])
     far = swap_y(near, 2)
     (acts,) = call(acts_kernel, [((T, FB), BF)], SHORT, after=1)(pos, *acts, near)
     own, one, two, three = call(

time: 163 us -> 160 us (0.982)
  starting transfers between devices: 50.6 us -> 48.3 us
    ppermute x10, waiting for transfers between devices: 37.9 us -> 28.6 us  [shift_zh(): lax.ppermute(value, 'wid', [(w, (w + 2 * step) % 8) for w in range(8)])]
    ppermute x2 -> x3, waiting for transfers between devices: 0.01 us -> 5.53 us  [swap_x(): return lax.ppermute(value, 'hid', [(h, h ^ 8 * bit) for h in range(32)])]
    ppermute x3, waiting for transfers between devices: 1.15 us -> 4.61 us  [shift_x(): lax.ppermute(value, 'hid', [(h, (h + 8 * step) % 32) for h in range(32)])]
    ppermute x10, starting transfers between devices: 23.4 us -> 20.2 us  [shift_zh(): lax.ppermute(value, 'wid', [(w, (w + 2 * step) % 8) for w in range(8)])]
    ppermute x3, waiting for transfers between devices: 5.41 us -> 8.41 us  [shift_y(): lax.ppermute(value, 'hid', [(h, h // 8 * 8 + (h % 8 + 2 * step) % 8) for...]
    all_to_all x1, starting transfers between devices: 4.02 us -> 6.46 us  [per_device(): lax.all_to_all(partial, 'hid', split_axis=0, concat_axis=0, tiled=True)]
    ppermute x2, starting transfers between devices: 7.38 us -> 5.04 us  [swap_y(): return lax.ppermute(value, 'hid', [(h, h ^ 2 * bit) for h in range(32)])]
    ppermute x2 -> x3, starting transfers between devices: 4.44 us -> 5.05 us  [swap_x(): return lax.ppermute(value, 'hid', [(h, h ^ 8 * bit) for h in range(32)])]
  transfers between devices with their start and end apart: 29 -> 30, of which waited for: 16 -> 20; matrix products, arithmetic and copies ran while one was open for 0% -> 0% of each run, Pallas kernels for 9% -> 9%
where the time goes in v2:
time: 160 us; the launch traced here: 159 us
  waiting for transfers between devices  78.3 us (49%)
  starting transfers between devices  48.3 us (30%)
  Pallas kernels  27.2 us (17%)
  local copies, waits for them, and re-layouts  4.35 us (3%)
    ppermute x10, waiting for transfers between devices, shift_zh(): lax.ppermute(value, 'wid', [(w, (w + 2 * step) % 8) for w in range(8)])  28.6 us
    pallas_call x10, Pallas kernels, run(): pl.pallas_call(body, out_shape=[(pltpu.HBM if o[2:] else jax.ShapeDtypeSt...  27.2 us
    all_to_all x1, waiting for transfers between devices, per_device(): lax.all_to_all(partial, 'hid', split_axis=0, concat_axis=0, tiled=True)  21 us
    ppermute x10, starting transfers between devices, shift_zh(): lax.ppermute(value, 'wid', [(w, (w + 2 * step) % 8) for w in range(8)])  20.2 us
    ppermute x3, waiting for transfers between devices, shift_y(): lax.ppermute(value, 'hid', [(h, h // 8 * 8 + (h % 8 + 2 * step) % 8) for...  8.41 us
    all_to_all x1, starting transfers between devices, per_device(): lax.all_to_all(partial, 'hid', split_axis=0, concat_axis=0, tiled=True)  6.46 us
    ppermute x3, waiting for transfers between devices, swap_x(): return lax.ppermute(value, 'hid', [(h, h ^ 8 * bit) for h in range(32)])  5.53 us
    ppermute x3, starting transfers between devices, swap_x(): return lax.ppermute(value, 'hid', [(h, h ^ 8 * bit) for h in range(32)])  5.05 us
  transfers between devices with their start and end apart: 30, of which 20 were waited for; matrix products, arithmetic and copies ran while one was open for 0% of the time, Pallas kernels for 9%

profile of v2, /device:TPU:64, one launch (start us, length us, event | category | flops | bytes accessed | tf_op | source)
XLA Modules:
  0.0 158.9 jit_solution(17059133545598498809)
XLA Ops:
  2.8 2.6 %collective-permute-done.1.refs_2_ = bf16[32,1024]{1,0:T(8,128)(2,1)S(1)} collective-permute-done((bf16[32,1024]{1,0:T(8,128)(2,1)}, bf16[32,1024]{1,0:T(8,128)(2,1)S(1)}, u32[]{:S(2)}, u32[]{:S(2)}) %collective-permute-start.1) | collective-permute-done | bytes 65568 | tf_op jit(solution)/shard_map/ppermute | solution.py:39
  9.2 4.0 %collective-permute-start.11 = (bf16[256,896]{1,0:T(8,128)(2,1)S(1)}, bf16[256,896]{1,0:T(8,128)(2,1)S(1)}, u32[]{:S(2)}, u32[]{:S(2)}) collective-permute-start(bf16[256,896]{1,0:T(8,128)(2,1)S(1)} %get-tuple-element.26.refs_1_), channel_id=1, source_target_pairs={{0,2},{1,3},{2,4},{3,5},{4,6},{5,7},{6,0},{7,1},{8,10},{9,11},{10,... | collective-permute-start | bytes 1376264 | tf_op jit(solution)/shard_map/ppermute | solution.py:43
  13.2 2.8 %collective-permute-start.4 = (bf16[64,1024]{1,0:T(8,128)(2,1)S(1)}, bf16[64,1024]{1,0:T(8,128)(2,1)S(1)}, u32[]{:S(2)}, u32[]{:S(2)}) collective-permute-start(bf16[64,1024]{1,0:T(8,128)(2,1)S(1)} %get-tuple-element.24.refs_1_), channel_id=1, source_target_pairs={{0,192},{8,200},{16,208},{24,216},{32,224},{40,232},{48,240},{56,2... | collective-permute-start | bytes 393224 | tf_op jit(solution)/shard_map/ppermute | solution.py:21
  17.6 2.5 %collective-permute-done.4.refs_4_ = bf16[64,1024]{1,0:T(8,128)(2,1)S(1)} collective-permute-done((bf16[64,1024]{1,0:T(8,128)(2,1)S(1)}, bf16[64,1024]{1,0:T(8,128)(2,1)S(1)}, u32[]{:S(2)}, u32[]{:S(2)}) %collective-permute-start.4) | collective-permute-done | bytes 131104 | tf_op jit(solution)/shard_map/ppermute | solution.py:21
  24.4 3.1 %collective-permute-start.7 = (bf16[256,1024]{1,0:T(8,128)(2,1)S(1)}, bf16[256,1024]{1,0:T(8,128)(2,1)S(1)}, u32[]{:S(2)}, u32[]{:S(2)}) collective-permute-start(bf16[256,1024]{1,0:T(8,128)(2,1)S(1)} %shard_map.103.refs_1_), channel_id=1, source_target_pairs={{0,48},{8,56},{16,0},{24,8},{32,16},{40,24},{48,32},{56,40},{64,11... | collective-permute-start | bytes 1572872 | tf_op jit(solution)/shard_map/ppermute | solution.py:25
  29.1 3.1 %collective-permute-done.13.refs_2_ = bf16[256,896]{1,0:T(8,128)(2,1)S(1)} collective-permute-done((bf16[256,896]{1,0:T(8,128)(2,1)S(1)}, bf16[256,896]{1,0:T(8,128)(2,1)S(1)}, u32[]{:S(2)}, u32[]{:S(2)}) %collective-permute-start.13) | collective-permute-done | bytes 458784 | tf_op jit(solution)/shard_map/ppermute | solution.py:43
  34.3 4.1 %collective-permute-done.9.refs_8_ = bf16[64,1024]{1,0:T(8,128)(2,1)S(1)} collective-permute-done((bf16[64,1024]{1,0:T(8,128)(2,1)S(1)}, bf16[64,1024]{1,0:T(8,128)(2,1)S(1)}, u32[]{:S(2)}, u32[]{:S(2)}) %collective-permute-start.9) | collective-permute-done | bytes 131104 | tf_op jit(solution)/shard_map/ppermute | solution.py:31
  39.8 2.7 %collective-permute-start.12 = (bf16[128,896]{1,0:T(8,128)(2,1)S(1)}, bf16[128,896]{1,0:T(8,128)(2,1)S(1)}, u32[]{:S(2)}, u32[]{:S(2)}) collective-permute-start(bf16[128,896]{1,0:T(8,128)(2,1)S(1)} %slice.8), channel_id=1, source_target_pairs={{0,2},{1,3},{2,4},{3,5},{4,6},{5,7},{6,0},{7,1},{8,10},{9,11},{10,... | collective-permute-start | bytes 688136 | tf_op jit(solution)/shard_map/ppermute | solution.py:43
  42.6 4.7 %collective-permute-done.7.refs_4_ = bf16[256,1024]{1,0:T(8,128)(2,1)S(1)} collective-permute-done((bf16[256,1024]{1,0:T(8,128)(2,1)S(1)}, bf16[256,1024]{1,0:T(8,128)(2,1)S(1)}, u32[]{:S(2)}, u32[]{:S(2)}) %collective-permute-start.7) | collective-permute-done | bytes 524320 | tf_op jit(solution)/shard_map/ppermute | solution.py:25
  47.3 3.7 %collective-permute-done.5.refs_2_ = bf16[256,1024]{1,0:T(8,128)(2,1)S(1)} collective-permute-done((bf16[256,1024]{1,0:T(8,128)(2,1)S(1)}, bf16[256,1024]{1,0:T(8,128)(2,1)S(1)}, u32[]{:S(2)}, u32[]{:S(2)}) %collective-permute-start.5) | collective-permute-done | bytes 524320 | tf_op jit(solution)/shard_map/ppermute | solution.py:25
  51.7 3.0 %shard_map.104 = (bf16[1024,1024]{1,0:T(8,128)(2,1)S(1)}, f32[512,896]{1,0:T(8,128)S(1)}, f32[512,896]{1,0:T(8,128)S(1)}, bf16[256,1024]{1,0:T(8,128)(2,1)S(1)}) custom-call(s32[5]{0:T(128)S(1)} %stack.23.refs_0_, bf16[256,1024]{1,0:T(8,128)(2,1)S(1)} %shard_map.103.refs_1_, bf16[256,1024]{1,0:T(8,128)(2,1)S(1)} %collective-permute-done.5.refs_2_, ...), custom_call_target="tpu_custom_call" | custom-call | flops 22548578304 | bytes 83886080 | tf_op jit(solution)/shard_map/pallas_call | solution.py:83
  54.8 3.5 %collective-permute-start.20 = (bf16[256,1024]{1,0:T(8,128)(2,1)S(1)}, bf16[256,1024]{1,0:T(8,128)(2,1)S(1)}, u32[]{:S(2)}, u32[]{:S(2)}) collective-permute-start(bf16[256,1024]{1,0:T(8,128)(2,1)S(1)} %get-tuple-element.33.refs_6_.refs_3_), channel_id=1, source_target_pairs={{0,32},{8,40},{16,48},{24,56},{32,0},{40,8},{48,16},{56,24},{64,96... | collective-permute-start | bytes 1572872 | tf_op jit(solution)/shard_map/ppermute | solution.py:35
  62.2 3.1 %collective-permute-start.17 = (bf16[128,896]{1,0:T(8,128)(2,1)S(1)}, bf16[128,896]{1,0:T(8,128)(2,1)S(1)}, u32[]{:S(2)}, u32[]{:S(2)}) collective-permute-start(bf16[128,896]{1,0:T(8,128)(2,1)S(1)} %get-tuple-element.31), channel_id=1, source_target_pairs={{0,4},{1,5},{2,6},{3,7},{4,0},{5,1},{6,2},{7,3},{8,12},{9,13},{10,... | collective-permute-start | bytes 688136 | tf_op jit(solution)/shard_map/ppermute | solution.py:43
  66.3 4.3 %collective-permute-done.20.refs_4_ = bf16[256,1024]{1,0:T(8,128)(2,1)S(1)} collective-permute-done((bf16[256,1024]{1,0:T(8,128)(2,1)S(1)}, bf16[256,1024]{1,0:T(8,128)(2,1)S(1)}, u32[]{:S(2)}, u32[]{:S(2)}) %collective-permute-start.20) | collective-permute-done | bytes 524320 | tf_op jit(solution)/shard_map/ppermute | solution.py:35
  70.7 4.9 %shard_map.107 = (bf16[896,1024]{1,0:T(8,128)(2,1)}, f32[1024,896]{1,0:T(8,128)S(1)}, f32[1024,896]{1,0:T(8,128)S(1)}, bf16[512,1024]{1,0:T(8,128)(2,1)S(1)}) custom-call(s32[5]{0:T(128)S(1)} %stack.23.refs_0_, bf16[1024,896]{1,0:T(8,128)(2,1)S(1)} %shard_map.106.refs_1_, bf16[1024,896]{1,0:T(8,128)(2,1)S(1)} %collective-permute-done.19.refs_2_, ...), custom_call_target="tpu_custom_call" | custom-call | flops 1879048192 | bytes 16777216 | tf_op jit(solution)/shard_map/pallas_call | solution.py:83
  75.6 3.0 %collective-permute-start.28 = (bf16[512,1024]{1,0:T(8,128)(2,1)S(1)}, bf16[512,1024]{1,0:T(8,128)(2,1)S(1)}, u32[]{:S(2)}, u32[]{:S(2)}) collective-permute-start(bf16[512,1024]{1,0:T(8,128)(2,1)S(1)} %get-tuple-element.37.refs_1_), channel_id=1, source_target_pairs={{0,128},{8,136},{16,144},{24,152},{32,160},{40,168},{48,176},{56,1... | collective-permute-start | bytes 3145736 | tf_op jit(solution)/shard_map/ppermute | solution.py:31
  78.6 7.1 %collective-permute-done.17.refs_3_ = bf16[128,896]{1,0:T(8,128)(2,1)S(1)} collective-permute-done((bf16[128,896]{1,0:T(8,128)(2,1)S(1)}, bf16[128,896]{1,0:T(8,128)(2,1)S(1)}, u32[]{:S(2)}, u32[]{:S(2)}) %collective-permute-start.17) | collective-permute-done | bytes 229408 | tf_op jit(solution)/shard_map/ppermute | solution.py:43
  87.4 2.8 %collective-permute-start.23 = (bf16[128,896]{1,0:T(8,128)(2,1)S(1)}, bf16[128,896]{1,0:T(8,128)(2,1)S(1)}, u32[]{:S(2)}, u32[]{:S(2)}) collective-permute-start(bf16[128,896]{1,0:T(8,128)(2,1)S(1)} %shard_map.108.refs_1_), channel_id=1, source_target_pairs={{0,2},{1,3},{2,4},{3,5},{4,6},{5,7},{6,0},{7,1},{8,10},{9,11},{10,... | collective-permute-start | bytes 688136 | tf_op jit(solution)/shard_map/ppermute | solution.py:43
  94.1 3.7 %collective-permute-done.23.refs_4_ = bf16[128,896]{1,0:T(8,128)(2,1)S(1)} collective-permute-done((bf16[128,896]{1,0:T(8,128)(2,1)S(1)}, bf16[128,896]{1,0:T(8,128)(2,1)S(1)}, u32[]{:S(2)}, u32[]{:S(2)}) %collective-permute-start.23) | collective-permute-done | bytes 229408 | tf_op jit(solution)/shard_map/ppermute | solution.py:43
  97.8 12.5 %collective-permute-done.22.refs_3_ = bf16[128,896]{1,0:T(8,128)(2,1)S(1)} collective-permute-done((bf16[128,896]{1,0:T(8,128)(2,1)S(1)}, bf16[128,896]{1,0:T(8,128)(2,1)S(1)}, u32[]{:S(2)}, u32[]{:S(2)}) %collective-permute-start.22) | collective-permute-done | bytes 229408 | tf_op jit(solution)/shard_map/ppermute | solution.py:43
  112.3 6.2 %shard_map.109 = (bf16[1024,1024]{1,0:T(8,128)(2,1)}, bf16[1024,896]{1,0:T(8,128)(2,1)}, bf16[1024,896]{1,0:T(8,128)(2,1)}) custom-call(s32[5]{0:T(128)S(1)} %stack.23.refs_0_, bf16[128,896]{1,0:T(8,128)(2,1)S(1)} %shard_map.108.refs_1_, bf16[128,896]{1,0:T(8,128)(2,1)S(1)} %collective-permute-done.21.refs_2_, ...), custom_call_target="tpu_custom_call" | custom-call | flops 3758096384 | bytes 15728640 | tf_op jit(solution)/shard_map/pallas_call | solution.py:83
  118.6 6.5 %all-to-all-start = ((bf16[32,32,1024]{2,1,0:T(8,128)(2,1)}), bf16[32,32,1024]{2,1,0:T(8,128)(2,1)S(1)}, u32[]{:S(2)}, u32[]{:S(2)}) async-start(bf16[32,32,1024]{2,1,0:T(8,128)(2,1)} %bitcast.6), calls=%async_computation | async-start | bytes 4194304 | tf_op jit(solution)/shard_map/all_to_all | solution.py:300
  129.3 7.1 %shard_map.111 = (bf16[1024,896]{1,0:T(8,128)(2,1)}, bf16[1024,896]{1,0:T(8,128)(2,1)}) custom-call(s32[5]{0:T(128)S(1)} %stack.23.refs_0_, bf16[512,1024]{1,0:T(8,128)(2,1)S(1)} %get-tuple-element.37.refs_1_, bf16[512,1024]{1,0:T(8,128)(2,1)S(1)} %copy-done.4, bf16[1024,896]{1,0:T(8,128)(2,1)S(1)} %copy-done.5, bf16[1024,896]{1,0:T(8,128)(2,1)S(1)} %copy-done.6), custom_call_target="tpu_custom_call" | custom-call | flops 3758096384 | bytes 10485760 | tf_op jit(solution)/shard_map/pallas_call | solution.py:83
  136.4 21.0 %all-to-all-done.refs_1_ = bf16[32,32,1024]{2,1,0:T(8,128)(2,1)S(1)} async-done(((bf16[32,32,1024]{2,1,0:T(8,128)(2,1)}), bf16[32,32,1024]{2,1,0:T(8,128)(2,1)S(1)}, u32[]{:S(2)}, u32[]{:S(2)}) %all-to-all-start) | async-done | bytes 2097184 | tf_op jit(solution)/shard_map/all_to_all | solution.py:300
  (63 shorter events, 35.9 us)
Async XLA Ops:
  9.0 23.3 %collective-permute-start.13 = (bf16[256,896]{1,0:T(8,128)(2,1)S(1)}, bf16[256,896]{1,0:T(8,128)(2,1)S(1)}, u32[]{:S(2)}, u32[]{:S(2)}) collective-permute-start(bf16[256,896]{1,0:T(8,128)(2,1)S(1)} %get-tuple-element.26.refs_1_), channel_id=1, source_target_pairs={{0,6},{1,7},{2,0},{3,1},{4,2},{5,3},{6,4},{7,5},{8,14},{9,15},{10,... | collective-permute-start | bytes 1376264 | tf_op jit(solution)/shard_map/ppermute | solution.py:43
  9.2 24.5 %collective-permute-start.11 = (bf16[256,896]{1,0:T(8,128)(2,1)S(1)}, bf16[256,896]{1,0:T(8,128)(2,1)S(1)}, u32[]{:S(2)}, u32[]{:S(2)}) collective-permute-start(bf16[256,896]{1,0:T(8,128)(2,1)S(1)} %get-tuple-element.26.refs_1_), channel_id=1, source_target_pairs={{0,2},{1,3},{2,4},{3,5},{4,6},{5,7},{6,0},{7,1},{8,10},{9,11},{10,... | collective-permute-start | bytes 1376264 | tf_op jit(solution)/shard_map/ppermute | solution.py:43
  13.2 7.0 %collective-permute-start.4 = (bf16[64,1024]{1,0:T(8,128)(2,1)S(1)}, bf16[64,1024]{1,0:T(8,128)(2,1)S(1)}, u32[]{:S(2)}, u32[]{:S(2)}) collective-permute-start(bf16[64,1024]{1,0:T(8,128)(2,1)S(1)} %get-tuple-element.24.refs_1_), channel_id=1, source_target_pairs={{0,192},{8,200},{16,208},{24,216},{32,224},{40,232},{48,240},{56,2... | collective-permute-start | bytes 393224 | tf_op jit(solution)/shard_map/ppermute | solution.py:21
  15.9 6.6 %collective-permute-start.3 = (bf16[64,1024]{1,0:T(8,128)(2,1)S(1)}, bf16[64,1024]{1,0:T(8,128)(2,1)S(1)}, u32[]{:S(2)}, u32[]{:S(2)}) collective-permute-start(bf16[64,1024]{1,0:T(8,128)(2,1)S(1)} %get-tuple-element.24.refs_1_), channel_id=1, source_target_pairs={{0,128},{8,136},{16,144},{24,152},{32,160},{40,168},{48,176},{56,1... | collective-permute-start | bytes 393224 | tf_op jit(solution)/shard_map/ppermute | solution.py:21
  16.7 7.1 %collective-permute-start.2 = (bf16[64,1024]{1,0:T(8,128)(2,1)S(1)}, bf16[64,1024]{1,0:T(8,128)(2,1)S(1)}, u32[]{:S(2)}, u32[]{:S(2)}) collective-permute-start(bf16[64,1024]{1,0:T(8,128)(2,1)S(1)} %get-tuple-element.24.refs_1_), channel_id=1, source_target_pairs={{0,64},{8,72},{16,80},{24,88},{32,96},{40,104},{48,112},{56,120},{... | collective-permute-start | bytes 393224 | tf_op jit(solution)/shard_map/ppermute | solution.py:21
  20.2 7.9 %collective-permute-start.8 = (bf16[64,1024]{1,0:T(8,128)(2,1)S(1)}, bf16[64,1024]{1,0:T(8,128)(2,1)S(1)}, u32[]{:S(2)}, u32[]{:S(2)}) collective-permute-start(bf16[64,1024]{1,0:T(8,128)(2,1)S(1)} %get-tuple-element.25.refs_6_), channel_id=1, source_target_pairs={{0,16},{8,24},{16,0},{24,8},{32,48},{40,56},{48,32},{56,40},{64,80... | collective-permute-start | bytes 393224 | tf_op jit(solution)/shard_map/ppermute | solution.py:35
  24.4 22.9 %collective-permute-start.7 = (bf16[256,1024]{1,0:T(8,128)(2,1)S(1)}, bf16[256,1024]{1,0:T(8,128)(2,1)S(1)}, u32[]{:S(2)}, u32[]{:S(2)}) collective-permute-start(bf16[256,1024]{1,0:T(8,128)(2,1)S(1)} %shard_map.103.refs_1_), channel_id=1, source_target_pairs={{0,48},{8,56},{16,0},{24,8},{32,16},{40,24},{48,32},{56,40},{64,11... | collective-permute-start | bytes 1572872 | tf_op jit(solution)/shard_map/ppermute | solution.py:25
  27.5 19.8 %collective-permute-start.6 = (bf16[256,1024]{1,0:T(8,128)(2,1)S(1)}, bf16[256,1024]{1,0:T(8,128)(2,1)S(1)}, u32[]{:S(2)}, u32[]{:S(2)}) collective-permute-start(bf16[256,1024]{1,0:T(8,128)(2,1)S(1)} %shard_map.103.refs_1_), channel_id=1, source_target_pairs={{0,32},{8,40},{16,48},{24,56},{32,0},{40,8},{48,16},{56,24},{64,96... | collective-permute-start | bytes 1572872 | tf_op jit(solution)/shard_map/ppermute | solution.py:25
  28.1 22.9 %collective-permute-start.5 = (bf16[256,1024]{1,0:T(8,128)(2,1)S(1)}, bf16[256,1024]{1,0:T(8,128)(2,1)S(1)}, u32[]{:S(2)}, u32[]{:S(2)}) collective-permute-start(bf16[256,1024]{1,0:T(8,128)(2,1)S(1)} %shard_map.103.refs_1_), channel_id=1, source_target_pairs={{0,16},{8,24},{16,32},{24,40},{32,48},{40,56},{48,0},{56,8},{64,80... | collective-permute-start | bytes 1572872 | tf_op jit(solution)/shard_map/ppermute | solution.py:25
  32.2 6.2 %collective-permute-start.9 = (bf16[64,1024]{1,0:T(8,128)(2,1)S(1)}, bf16[64,1024]{1,0:T(8,128)(2,1)S(1)}, u32[]{:S(2)}, u32[]{:S(2)}) collective-permute-start(bf16[64,1024]{1,0:T(8,128)(2,1)S(1)} %get-tuple-element.25.refs_6_), channel_id=1, source_target_pairs={{0,64},{8,72},{16,80},{24,88},{32,96},{40,104},{48,112},{56,120},{... | collective-permute-start | bytes 393224 | tf_op jit(solution)/shard_map/ppermute | solution.py:31
  38.4 12.6 %collective-permute-start.14 = (bf16[128,896]{1,0:T(8,128)(2,1)S(1)}, bf16[128,896]{1,0:T(8,128)(2,1)S(1)}, u32[]{:S(2)}, u32[]{:S(2)}) collective-permute-start(bf16[128,896]{1,0:T(8,128)(2,1)S(1)} %slice.9), channel_id=1, source_target_pairs={{0,6},{1,7},{2,0},{3,1},{4,2},{5,3},{6,4},{7,5},{8,14},{9,15},{10,... | collective-permute-start | bytes 688136 | tf_op jit(solution)/shard_map/ppermute | solution.py:43
  39.8 11.8 %collective-permute-start.12 = (bf16[128,896]{1,0:T(8,128)(2,1)S(1)}, bf16[128,896]{1,0:T(8,128)(2,1)S(1)}, u32[]{:S(2)}, u32[]{:S(2)}) collective-permute-start(bf16[128,896]{1,0:T(8,128)(2,1)S(1)} %slice.8), channel_id=1, source_target_pairs={{0,2},{1,3},{2,4},{3,5},{4,6},{5,7},{6,0},{7,1},{8,10},{9,11},{10,... | collective-permute-start | bytes 688136 | tf_op jit(solution)/shard_map/ppermute | solution.py:43
  54.8 15.8 %collective-permute-start.20 = (bf16[256,1024]{1,0:T(8,128)(2,1)S(1)}, bf16[256,1024]{1,0:T(8,128)(2,1)S(1)}, u32[]{:S(2)}, u32[]{:S(2)}) collective-permute-start(bf16[256,1024]{1,0:T(8,128)(2,1)S(1)} %get-tuple-element.33.refs_6_.refs_3_), channel_id=1, source_target_pairs={{0,32},{8,40},{16,48},{24,56},{32,0},{40,8},{48,16},{56,24},{64,96... | collective-permute-start | bytes 1572872 | tf_op jit(solution)/shard_map/ppermute | solution.py:35
  59.0 11.7 %collective-permute-start.19 = (bf16[1024,896]{1,0:T(8,128)(2,1)S(1)}, bf16[1024,896]{1,0:T(8,128)(2,1)S(1)}, u32[]{:S(2)}, u32[]{:S(2)}) collective-permute-start(bf16[1024,896]{1,0:T(8,128)(2,1)S(1)} %shard_map.106.refs_1_), channel_id=1, source_target_pairs={{0,1},{1,0},{2,3},{3,2},{4,5},{5,4},{6,7},{7,6},{8,9},{9,8},{10,11... | collective-permute-start | bytes 5505032 | tf_op jit(solution)/shard_map/ppermute | solution.py:47
  59.8 18.8 %collective-permute-start.16 = (bf16[128,896]{1,0:T(8,128)(2,1)S(1)}, bf16[128,896]{1,0:T(8,128)(2,1)S(1)}, u32[]{:S(2)}, u32[]{:S(2)}) collective-permute-start(bf16[128,896]{1,0:T(8,128)(2,1)S(1)} %get-tuple-element.30), channel_id=1, source_target_pairs={{0,2},{1,3},{2,4},{3,5},{4,6},{5,7},{6,0},{7,1},{8,10},{9,11},{10,... | collective-permute-start | bytes 688136 | tf_op jit(solution)/shard_map/ppermute | solution.py:43
  62.2 23.4 %collective-permute-start.17 = (bf16[128,896]{1,0:T(8,128)(2,1)S(1)}, bf16[128,896]{1,0:T(8,128)(2,1)S(1)}, u32[]{:S(2)}, u32[]{:S(2)}) collective-permute-start(bf16[128,896]{1,0:T(8,128)(2,1)S(1)} %get-tuple-element.31), channel_id=1, source_target_pairs={{0,4},{1,5},{2,6},{3,7},{4,0},{5,1},{6,2},{7,3},{8,12},{9,13},{10,... | collective-permute-start | bytes 688136 | tf_op jit(solution)/shard_map/ppermute | solution.py:43
  65.4 21.3 %collective-permute-start.18 = (bf16[128,896]{1,0:T(8,128)(2,1)S(1)}, bf16[128,896]{1,0:T(8,128)(2,1)S(1)}, u32[]{:S(2)}, u32[]{:S(2)}) collective-permute-start(bf16[128,896]{1,0:T(8,128)(2,1)S(1)} %get-tuple-element.32), channel_id=1, source_target_pairs={{0,6},{1,7},{2,0},{3,1},{4,2},{5,3},{6,4},{7,5},{8,14},{9,15},{10,... | collective-permute-start | bytes 688136 | tf_op jit(solution)/shard_map/ppermute | solution.py:43
  75.6 36.8 %collective-permute-start.28 = (bf16[512,1024]{1,0:T(8,128)(2,1)S(1)}, bf16[512,1024]{1,0:T(8,128)(2,1)S(1)}, u32[]{:S(2)}, u32[]{:S(2)}) collective-permute-start(bf16[512,1024]{1,0:T(8,128)(2,1)S(1)} %get-tuple-element.37.refs_1_), channel_id=1, source_target_pairs={{0,128},{8,136},{16,144},{24,152},{32,160},{40,168},{48,176},{56,1... | collective-permute-start | bytes 3145736 | tf_op jit(solution)/shard_map/ppermute | solution.py:31
  87.4 10.4 %collective-permute-start.23 = (bf16[128,896]{1,0:T(8,128)(2,1)S(1)}, bf16[128,896]{1,0:T(8,128)(2,1)S(1)}, u32[]{:S(2)}, u32[]{:S(2)}) collective-permute-start(bf16[128,896]{1,0:T(8,128)(2,1)S(1)} %shard_map.108.refs_1_), channel_id=1, source_target_pairs={{0,2},{1,3},{2,4},{3,5},{4,6},{5,7},{6,0},{7,1},{8,10},{9,11},{10,... | collective-permute-start | bytes 688136 | tf_op jit(solution)/shard_map/ppermute | solution.py:43
  90.2 20.1 %collective-permute-start.22 = (bf16[128,896]{1,0:T(8,128)(2,1)S(1)}, bf16[128,896]{1,0:T(8,128)(2,1)S(1)}, u32[]{:S(2)}, u32[]{:S(2)}) collective-permute-start(bf16[128,896]{1,0:T(8,128)(2,1)S(1)} %shard_map.108.refs_1_), channel_id=1, source_target_pairs={{0,4},{1,5},{2,6},{3,7},{4,0},{5,1},{6,2},{7,3},{8,12},{9,13},{10,... | collective-permute-start | bytes 688136 | tf_op jit(solution)/shard_map/ppermute | solution.py:43
  92.4 18.5 %collective-permute-start.21 = (bf16[128,896]{1,0:T(8,128)(2,1)S(1)}, bf16[128,896]{1,0:T(8,128)(2,1)S(1)}, u32[]{:S(2)}, u32[]{:S(2)}) collective-permute-start(bf16[128,896]{1,0:T(8,128)(2,1)S(1)} %shard_map.108.refs_1_), channel_id=1, source_target_pairs={{0,6},{1,7},{2,0},{3,1},{4,2},{5,3},{6,4},{7,5},{8,14},{9,15},{10,... | collective-permute-start | bytes 688136 | tf_op jit(solution)/shard_map/ppermute | solution.py:43
  94.1 16.7 %collective-permute-start.24 = (bf16[128,896]{1,0:T(8,128)(2,1)S(1)}, bf16[128,896]{1,0:T(8,128)(2,1)S(1)}, u32[]{:S(2)}, u32[]{:S(2)}) collective-permute-start(bf16[128,896]{1,0:T(8,128)(2,1)S(1)} %shard_map.108.refs_1_), channel_id=1, source_target_pairs={{0,1},{1,0},{2,3},{3,2},{4,5},{5,4},{6,7},{7,6},{8,9},{9,8},{10,11... | collective-permute-start | bytes 688136 | tf_op jit(solution)/shard_map/ppermute | solution.py:47
  97.8 13.1 %collective-permute-start.27 = (bf16[128,896]{1,0:T(8,128)(2,1)S(1)}, bf16[128,896]{1,0:T(8,128)(2,1)S(1)}, u32[]{:S(2)}, u32[]{:S(2)}) collective-permute-start(bf16[128,896]{1,0:T(8,128)(2,1)S(1)} %collective-permute-done.23.refs_4_), channel_id=1, source_target_pairs={{0,1},{1,0},{2,3},{3,2},{4,5},{5,4},{6,7},{7,6},{8,9},{9,8},{10,11... | collective-permute-start | bytes 688136 | tf_op jit(solution)/shard_map/ppermute | solution.py:47
  118.6 38.8 %all-to-all-start = ((bf16[32,32,1024]{2,1,0:T(8,128)(2,1)}), bf16[32,32,1024]{2,1,0:T(8,128)(2,1)S(1)}, u32[]{:S(2)}, u32[]{:S(2)}) async-start(bf16[32,32,1024]{2,1,0:T(8,128)(2,1)} %bitcast.6), calls=%async_computation | async-start | bytes 4194304 | tf_op jit(solution)/shard_map/all_to_all | solution.py:300
  (13 other events, 135.5 us)

commit v3 on v2

--- a/solution.py
+++ b/solution.py
@@ -125,17 +125,25 @@
         refs[4][i * 64 : (i + 1) * 64] = part[...]
 
 
-def hidden_grad_kernel(pos, *refs):
-    pieces, w_down, rows, (grads, keep, send, rows_out) = refs[:4], refs[4], refs[5:9], refs[9:]
-    for j, piece in enumerate(pieces):
-        to_local(pos, piece, grads, lambda k, j=j: ((pos[0] - k) & 3, (pos[1] - j) & 3))
+def hidden_grad(grads, w_down, out):
     for start, width in COL_TILES:
         cols = slice(start, start + width)
-        part = dot_nt(grads[...], w_down[cols, :])
-        keep[:, cols] = part[:512]
-        send[:, cols] = part[512:]
+        out[:, cols] = dot_nt(grads[...], w_down[cols, :])
+
+
+def send_kernel(pos, *refs):
+    pieces, w_down, rows, (own, other, send, rows_out, local) = refs[:4], refs[4], refs[5:9], refs[9:]
+    for j, piece in enumerate(pieces):
+        to_local(pos, piece, local, lambda k, j=j: ((pos[0] - k) & 3, (pos[1] - j) & 3))
+    own[...] = local[:512]
+    other[...] = local[512:]
+    hidden_grad(other, w_down, send)
     for i, part in enumerate(rows):
         rows_out[i * 64 : (i + 1) * 64] = part[...]
+
+
+def keep_kernel(pos, own, w_down, keep):
+    hidden_grad(own, w_down, keep)
 
 
 def acts_kernel(pos, here, below, above, far_gate, far_up, out):
@@ -159,7 +167,7 @@
 
 
 def down_kernel(pos, *refs):
-    blocks, near, far, grads, out, act_out, slope_out, rows_out, hidden = refs[:2], *refs[2:]
+    blocks, near, far, own, other, out, act_out, slope_out, rows_out, hidden = refs[:2], *refs[2:]
     rows_out[:256] = near[...]
     rows_out[256:] = far[...]
     for i in range(8):
@@ -174,7 +182,8 @@
         hidden[rows] = (act * up).astype(BF)
     for start in range(0, DB, 256):
         cols = slice(start, start + 256)
-        out[:, cols] = dot_tn(hidden[...], grads[:, cols]).astype(BF)
+        total = dot_tn(hidden[:512], own[:, cols]) + dot_tn(hidden[512:], other[:, cols])
+        out[:, cols] = total.astype(BF)
 
 
 def sum_kernel(pos, parts, out):
@@ -264,12 +273,14 @@
     )
     near = [near, swap_y(near, 1)]
     near += [swap_x(part, 1) for part in near]
-    all_grads, keep, send, near = call(
-        hidden_grad_kernel,
-        [((T, DB), BF), ((512, FB), F32), ((512, FB), F32), ((256, DB), BF)],
+    own_grads, other_grads, send, near = call(
+        send_kernel,
+        [((512, DB), BF), ((512, DB), BF), ((512, FB), F32), ((256, DB), BF)],
         LONG,
+        [pltpu.VMEM((T, DB), BF)],
         after=2,
     )(pos, block, *[shift_y(block, k) for k in (1, 2, 3)], w_down, *near, *acts[3:])
+    (keep,) = call(keep_kernel, [((512, FB), F32)], (MM // 2, 4 * MB))(pos, own_grads, w_down)
     far = swap_y(near, 2)
     (acts,) = call(acts_kernel, [((T, FB), BF)], SHORT, after=1)(pos, *acts, near)
     own, one, two, three = call(
@@ -281,7 +292,7 @@
         [((FB, DB), BF), ((T, FB), F32), ((T, FB), F32), ((512, DB), BF)],
         (MM, 16 * MB),
         [pltpu.VMEM((T, FB), BF)],
-    )(pos, acts, swap_core(acts), near, far, all_grads)
+    )(pos, acts, swap_core(acts), near, far, own_grads, other_grads)
     far = swap_x(near, 2)
     (hg,) = call(ring_sum_kernel, [((128, FB), BF)], LONG, after=1)(pos, own, *got, act)
     hgs = spread_core(gather_zh(hg))

time: 160 us -> 160 us (level)
  starting transfers between devices: 48.3 us -> 46 us
    ppermute x10, waiting for transfers between devices: 28.6 us -> 30.5 us  [shift_zh(): lax.ppermute(value, 'wid', [(w, (w + 2 * step) % 8) for w in range(8)])]
    pallas_call x10 -> x11, Pallas kernels: 27.2 us -> 27.9 us  [run(): pl.pallas_call(body, out_shape=[(pltpu.HBM if o[2:] else jax.ShapeDtypeSt...]
  transfers between devices with their start and end apart: 30 -> 30, of which waited for: 20 -> 20; matrix products, arithmetic and copies ran while one was open for 0% -> 0% of each run, Pallas kernels for 9% -> 10%
where the time goes in v3:
time: 160 us; the launch traced here: 158 us
  waiting for transfers between devices  79.3 us (50%)
  starting transfers between devices  46 us (29%)
  Pallas kernels  27.9 us (17%)
  local copies, waits for them, and re-layouts  4.35 us (3%)
    ppermute x10, waiting for transfers between devices, shift_zh(): lax.ppermute(value, 'wid', [(w, (w + 2 * step) % 8) for w in range(8)])  30.5 us
    pallas_call x11, Pallas kernels, run(): pl.pallas_call(body, out_shape=[(pltpu.HBM if o[2:] else jax.ShapeDtypeSt...  27.9 us
    all_to_all x1, waiting for transfers between devices, per_device(): lax.all_to_all(partial, 'hid', split_axis=0, concat_axis=0, tiled=True)  21 us
    ppermute x10, starting transfers between devices, shift_zh(): lax.ppermute(value, 'wid', [(w, (w + 2 * step) % 8) for w in range(8)])  19.3 us
    ppermute x3, waiting for transfers between devices, shift_y(): lax.ppermute(value, 'hid', [(h, h // 8 * 8 + (h % 8 + 2 * step) % 8) for...  8.41 us
    ppermute x3, waiting for transfers between devices, swap_x(): return lax.ppermute(value, 'hid', [(h, h ^ 8 * bit) for h in range(32)])  5.53 us
    all_to_all x1, starting transfers between devices, per_device(): lax.all_to_all(partial, 'hid', split_axis=0, concat_axis=0, tiled=True)  5.17 us
    ppermute x3, starting transfers between devices, swap_x(): return lax.ppermute(value, 'hid', [(h, h ^ 8 * bit) for h in range(32)])  5.05 us
  transfers between devices with their start and end apart: 30, of which 20 were waited for; matrix products, arithmetic and copies ran while one was open for 0% of the time, Pallas kernels for 10%

profile of v3, /device:TPU:64, one launch (start us, length us, event | category | flops | bytes accessed | tf_op | source)
XLA Modules:
  0.0 158.4 jit_solution(16875997188693422550)
XLA Ops:
  2.8 2.6 %collective-permute-done.1.refs_2_ = bf16[32,1024]{1,0:T(8,128)(2,1)S(1)} collective-permute-done((bf16[32,1024]{1,0:T(8,128)(2,1)}, bf16[32,1024]{1,0:T(8,128)(2,1)S(1)}, u32[]{:S(2)}, u32[]{:S(2)}) %collective-permute-start.1) | collective-permute-done | bytes 65568 | tf_op jit(solution)/shard_map/ppermute | solution.py:39
  9.2 4.0 %collective-permute-start.11 = (bf16[256,896]{1,0:T(8,128)(2,1)S(1)}, bf16[256,896]{1,0:T(8,128)(2,1)S(1)}, u32[]{:S(2)}, u32[]{:S(2)}) collective-permute-start(bf16[256,896]{1,0:T(8,128)(2,1)S(1)} %get-tuple-element.26.refs_1_), channel_id=1, source_target_pairs={{0,2},{1,3},{2,4},{3,5},{4,6},{5,7},{6,0},{7,1},{8,10},{9,11},{10,... | collective-permute-start | bytes 1376264 | tf_op jit(solution)/shard_map/ppermute | solution.py:43
  13.2 2.8 %collective-permute-start.4 = (bf16[64,1024]{1,0:T(8,128)(2,1)S(1)}, bf16[64,1024]{1,0:T(8,128)(2,1)S(1)}, u32[]{:S(2)}, u32[]{:S(2)}) collective-permute-start(bf16[64,1024]{1,0:T(8,128)(2,1)S(1)} %get-tuple-element.24.refs_1_), channel_id=1, source_target_pairs={{0,192},{8,200},{16,208},{24,216},{32,224},{40,232},{48,240},{56,2... | collective-permute-start | bytes 393224 | tf_op jit(solution)/shard_map/ppermute | solution.py:21
  17.6 2.5 %collective-permute-done.4.refs_4_ = bf16[64,1024]{1,0:T(8,128)(2,1)S(1)} collective-permute-done((bf16[64,1024]{1,0:T(8,128)(2,1)S(1)}, bf16[64,1024]{1,0:T(8,128)(2,1)S(1)}, u32[]{:S(2)}, u32[]{:S(2)}) %collective-permute-start.4) | collective-permute-done | bytes 131104 | tf_op jit(solution)/shard_map/ppermute | solution.py:21
  24.4 3.1 %collective-permute-start.7 = (bf16[256,1024]{1,0:T(8,128)(2,1)S(1)}, bf16[256,1024]{1,0:T(8,128)(2,1)S(1)}, u32[]{:S(2)}, u32[]{:S(2)}) collective-permute-start(bf16[256,1024]{1,0:T(8,128)(2,1)S(1)} %shard_map.103.refs_1_), channel_id=1, source_target_pairs={{0,48},{8,56},{16,0},{24,8},{32,16},{40,24},{48,32},{56,40},{64,11... | collective-permute-start | bytes 1572872 | tf_op jit(solution)/shard_map/ppermute | solution.py:25
  29.1 3.1 %collective-permute-done.13.refs_2_ = bf16[256,896]{1,0:T(8,128)(2,1)S(1)} collective-permute-done((bf16[256,896]{1,0:T(8,128)(2,1)S(1)}, bf16[256,896]{1,0:T(8,128)(2,1)S(1)}, u32[]{:S(2)}, u32[]{:S(2)}) %collective-permute-start.13) | collective-permute-done | bytes 458784 | tf_op jit(solution)/shard_map/ppermute | solution.py:43
  34.3 4.1 %collective-permute-done.9.refs_8_ = bf16[64,1024]{1,0:T(8,128)(2,1)S(1)} collective-permute-done((bf16[64,1024]{1,0:T(8,128)(2,1)S(1)}, bf16[64,1024]{1,0:T(8,128)(2,1)S(1)}, u32[]{:S(2)}, u32[]{:S(2)}) %collective-permute-start.9) | collective-permute-done | bytes 131104 | tf_op jit(solution)/shard_map/ppermute | solution.py:31
  39.8 2.7 %collective-permute-start.12 = (bf16[128,896]{1,0:T(8,128)(2,1)S(1)}, bf16[128,896]{1,0:T(8,128)(2,1)S(1)}, u32[]{:S(2)}, u32[]{:S(2)}) collective-permute-start(bf16[128,896]{1,0:T(8,128)(2,1)S(1)} %slice.8), channel_id=1, source_target_pairs={{0,2},{1,3},{2,4},{3,5},{4,6},{5,7},{6,0},{7,1},{8,10},{9,11},{10,... | collective-permute-start | bytes 688136 | tf_op jit(solution)/shard_map/ppermute | solution.py:43
  42.6 4.7 %collective-permute-done.7.refs_4_ = bf16[256,1024]{1,0:T(8,128)(2,1)S(1)} collective-permute-done((bf16[256,1024]{1,0:T(8,128)(2,1)S(1)}, bf16[256,1024]{1,0:T(8,128)(2,1)S(1)}, u32[]{:S(2)}, u32[]{:S(2)}) %collective-permute-start.7) | collective-permute-done | bytes 524320 | tf_op jit(solution)/shard_map/ppermute | solution.py:25
  47.3 3.7 %collective-permute-done.5.refs_2_ = bf16[256,1024]{1,0:T(8,128)(2,1)S(1)} collective-permute-done((bf16[256,1024]{1,0:T(8,128)(2,1)S(1)}, bf16[256,1024]{1,0:T(8,128)(2,1)S(1)}, u32[]{:S(2)}, u32[]{:S(2)}) %collective-permute-start.5) | collective-permute-done | bytes 524320 | tf_op jit(solution)/shard_map/ppermute | solution.py:25
  53.8 3.5 %collective-permute-start.20 = (bf16[256,1024]{1,0:T(8,128)(2,1)S(1)}, bf16[256,1024]{1,0:T(8,128)(2,1)S(1)}, u32[]{:S(2)}, u32[]{:S(2)}) collective-permute-start(bf16[256,1024]{1,0:T(8,128)(2,1)S(1)} %get-tuple-element.33.refs_6_.refs_3_), channel_id=1, source_target_pairs={{0,32},{8,40},{16,48},{24,56},{32,0},{40,8},{48,16},{56,24},{64,96... | collective-permute-start | bytes 1572872 | tf_op jit(solution)/shard_map/ppermute | solution.py:35
  60.6 2.4 %collective-permute-start.16 = (bf16[128,896]{1,0:T(8,128)(2,1)S(1)}, bf16[128,896]{1,0:T(8,128)(2,1)S(1)}, u32[]{:S(2)}, u32[]{:S(2)}) collective-permute-start(bf16[128,896]{1,0:T(8,128)(2,1)S(1)} %get-tuple-element.30), channel_id=1, source_target_pairs={{0,2},{1,3},{2,4},{3,5},{4,6},{5,7},{6,0},{7,1},{8,10},{9,11},{10,... | collective-permute-start | bytes 688136 | tf_op jit(solution)/shard_map/ppermute | solution.py:43
  63.0 3.1 %collective-permute-start.17 = (bf16[128,896]{1,0:T(8,128)(2,1)S(1)}, bf16[128,896]{1,0:T(8,128)(2,1)S(1)}, u32[]{:S(2)}, u32[]{:S(2)}) collective-permute-start(bf16[128,896]{1,0:T(8,128)(2,1)S(1)} %get-tuple-element.31), channel_id=1, source_target_pairs={{0,4},{1,5},{2,6},{3,7},{4,0},{5,1},{6,2},{7,3},{8,12},{9,13},{10,... | collective-permute-start | bytes 688136 | tf_op jit(solution)/shard_map/ppermute | solution.py:43
  66.2 3.4 %collective-permute-done.20.refs_4_ = bf16[256,1024]{1,0:T(8,128)(2,1)S(1)} collective-permute-done((bf16[256,1024]{1,0:T(8,128)(2,1)S(1)}, bf16[256,1024]{1,0:T(8,128)(2,1)S(1)}, u32[]{:S(2)}, u32[]{:S(2)}) %collective-permute-start.20) | collective-permute-done | bytes 524320 | tf_op jit(solution)/shard_map/ppermute | solution.py:35
  69.6 4.9 %shard_map.108 = (bf16[896,1024]{1,0:T(8,128)(2,1)}, f32[1024,896]{1,0:T(8,128)S(1)}, f32[1024,896]{1,0:T(8,128)S(1)}, bf16[512,1024]{1,0:T(8,128)(2,1)S(1)}) custom-call(s32[5]{0:T(128)S(1)} %stack.23.refs_0_, bf16[1024,896]{1,0:T(8,128)(2,1)S(1)} %shard_map.107.refs_1_, bf16[1024,896]{1,0:T(8,128)(2,1)S(1)} %collective-permute-done.19.refs_2_, ...), custom_call_target="tpu_custom_call" | custom-call | flops 1879048192 | bytes 16777216 | tf_op jit(solution)/shard_map/pallas_call | solution.py:83
  74.5 3.0 %collective-permute-start.28 = (bf16[512,1024]{1,0:T(8,128)(2,1)S(1)}, bf16[512,1024]{1,0:T(8,128)(2,1)S(1)}, u32[]{:S(2)}, u32[]{:S(2)}) collective-permute-start(bf16[512,1024]{1,0:T(8,128)(2,1)S(1)} %get-tuple-element.37.refs_1_), channel_id=1, source_target_pairs={{0,128},{8,136},{16,144},{24,152},{32,160},{40,168},{48,176},{56,1... | collective-permute-start | bytes 3145736 | tf_op jit(solution)/shard_map/ppermute | solution.py:31
  77.5 9.4 %collective-permute-done.17.refs_3_ = bf16[128,896]{1,0:T(8,128)(2,1)S(1)} collective-permute-done((bf16[128,896]{1,0:T(8,128)(2,1)S(1)}, bf16[128,896]{1,0:T(8,128)(2,1)S(1)}, u32[]{:S(2)}, u32[]{:S(2)}) %collective-permute-start.17) | collective-permute-done | bytes 229408 | tf_op jit(solution)/shard_map/ppermute | solution.py:43
  88.1 2.9 %collective-permute-start.23 = (bf16[128,896]{1,0:T(8,128)(2,1)S(1)}, bf16[128,896]{1,0:T(8,128)(2,1)S(1)}, u32[]{:S(2)}, u32[]{:S(2)}) collective-permute-start(bf16[128,896]{1,0:T(8,128)(2,1)S(1)} %shard_map.109.refs_1_), channel_id=1, source_target_pairs={{0,2},{1,3},{2,4},{3,5},{4,6},{5,7},{6,0},{7,1},{8,10},{9,11},{10,... | collective-permute-start | bytes 688136 | tf_op jit(solution)/shard_map/ppermute | solution.py:43
  94.9 3.6 %collective-permute-done.23.refs_4_ = bf16[128,896]{1,0:T(8,128)(2,1)S(1)} collective-permute-done((bf16[128,896]{1,0:T(8,128)(2,1)S(1)}, bf16[128,896]{1,0:T(8,128)(2,1)S(1)}, u32[]{:S(2)}, u32[]{:S(2)}) %collective-permute-start.23) | collective-permute-done | bytes 229408 | tf_op jit(solution)/shard_map/ppermute | solution.py:43
  98.5 12.6 %collective-permute-done.22.refs_3_ = bf16[128,896]{1,0:T(8,128)(2,1)S(1)} collective-permute-done((bf16[128,896]{1,0:T(8,128)(2,1)S(1)}, bf16[128,896]{1,0:T(8,128)(2,1)S(1)}, u32[]{:S(2)}, u32[]{:S(2)}) %collective-permute-start.22) | collective-permute-done | bytes 229408 | tf_op jit(solution)/shard_map/ppermute | solution.py:43
  113.1 6.2 %shard_map.110 = (bf16[1024,1024]{1,0:T(8,128)(2,1)}, bf16[1024,896]{1,0:T(8,128)(2,1)}, bf16[1024,896]{1,0:T(8,128)(2,1)}) custom-call(s32[5]{0:T(128)S(1)} %stack.23.refs_0_, bf16[128,896]{1,0:T(8,128)(2,1)S(1)} %shard_map.109.refs_1_, bf16[128,896]{1,0:T(8,128)(2,1)S(1)} %collective-permute-done.21.refs_2_, ...), custom_call_target="tpu_custom_call" | custom-call | flops 3758096384 | bytes 15728640 | tf_op jit(solution)/shard_map/pallas_call | solution.py:83
  119.4 5.2 %all-to-all-start = ((bf16[32,32,1024]{2,1,0:T(8,128)(2,1)}), bf16[32,32,1024]{2,1,0:T(8,128)(2,1)S(1)}, u32[]{:S(2)}, u32[]{:S(2)}) async-start(bf16[32,32,1024]{2,1,0:T(8,128)(2,1)} %bitcast.6), calls=%async_computation | async-start | bytes 4194304 | tf_op jit(solution)/shard_map/all_to_all | solution.py:311
  128.8 7.1 %shard_map.112 = (bf16[1024,896]{1,0:T(8,128)(2,1)}, bf16[1024,896]{1,0:T(8,128)(2,1)}) custom-call(s32[5]{0:T(128)S(1)} %stack.23.refs_0_, bf16[512,1024]{1,0:T(8,128)(2,1)S(1)} %get-tuple-element.37.refs_1_, bf16[512,1024]{1,0:T(8,128)(2,1)S(1)} %copy-done.4, bf16[1024,896]{1,0:T(8,128)(2,1)S(1)} %copy-done.5, bf16[1024,896]{1,0:T(8,128)(2,1)S(1)} %copy-done.6), custom_call_target="tpu_custom_call" | custom-call | flops 3758096384 | bytes 10485760 | tf_op jit(solution)/shard_map/pallas_call | solution.py:83
  135.9 21.0 %all-to-all-done.refs_1_ = bf16[32,32,1024]{2,1,0:T(8,128)(2,1)S(1)} async-done(((bf16[32,32,1024]{2,1,0:T(8,128)(2,1)}), bf16[32,32,1024]{2,1,0:T(8,128)(2,1)S(1)}, u32[]{:S(2)}, u32[]{:S(2)}) %all-to-all-start) | async-done | bytes 2097184 | tf_op jit(solution)/shard_map/all_to_all | solution.py:311
  (64 shorter events, 35.8 us)
Async XLA Ops:
  9.0 23.3 %collective-permute-start.13 = (bf16[256,896]{1,0:T(8,128)(2,1)S(1)}, bf16[256,896]{1,0:T(8,128)(2,1)S(1)}, u32[]{:S(2)}, u32[]{:S(2)}) collective-permute-start(bf16[256,896]{1,0:T(8,128)(2,1)S(1)} %get-tuple-element.26.refs_1_), channel_id=1, source_target_pairs={{0,6},{1,7},{2,0},{3,1},{4,2},{5,3},{6,4},{7,5},{8,14},{9,15},{10,... | collective-permute-start | bytes 1376264 | tf_op jit(solution)/shard_map/ppermute | solution.py:43
  9.2 24.5 %collective-permute-start.11 = (bf16[256,896]{1,0:T(8,128)(2,1)S(1)}, bf16[256,896]{1,0:T(8,128)(2,1)S(1)}, u32[]{:S(2)}, u32[]{:S(2)}) collective-permute-start(bf16[256,896]{1,0:T(8,128)(2,1)S(1)} %get-tuple-element.26.refs_1_), channel_id=1, source_target_pairs={{0,2},{1,3},{2,4},{3,5},{4,6},{5,7},{6,0},{7,1},{8,10},{9,11},{10,... | collective-permute-start | bytes 1376264 | tf_op jit(solution)/shard_map/ppermute | solution.py:43
  13.2 7.0 %collective-permute-start.4 = (bf16[64,1024]{1,0:T(8,128)(2,1)S(1)}, bf16[64,1024]{1,0:T(8,128)(2,1)S(1)}, u32[]{:S(2)}, u32[]{:S(2)}) collective-permute-start(bf16[64,1024]{1,0:T(8,128)(2,1)S(1)} %get-tuple-element.24.refs_1_), channel_id=1, source_target_pairs={{0,192},{8,200},{16,208},{24,216},{32,224},{40,232},{48,240},{56,2... | collective-permute-start | bytes 393224 | tf_op jit(solution)/shard_map/ppermute | solution.py:21
  15.9 6.6 %collective-permute-start.3 = (bf16[64,1024]{1,0:T(8,128)(2,1)S(1)}, bf16[64,1024]{1,0:T(8,128)(2,1)S(1)}, u32[]{:S(2)}, u32[]{:S(2)}) collective-permute-start(bf16[64,1024]{1,0:T(8,128)(2,1)S(1)} %get-tuple-element.24.refs_1_), channel_id=1, source_target_pairs={{0,128},{8,136},{16,144},{24,152},{32,160},{40,168},{48,176},{56,1... | collective-permute-start | bytes 393224 | tf_op jit(solution)/shard_map/ppermute | solution.py:21
  16.7 7.1 %collective-permute-start.2 = (bf16[64,1024]{1,0:T(8,128)(2,1)S(1)}, bf16[64,1024]{1,0:T(8,128)(2,1)S(1)}, u32[]{:S(2)}, u32[]{:S(2)}) collective-permute-start(bf16[64,1024]{1,0:T(8,128)(2,1)S(1)} %get-tuple-element.24.refs_1_), channel_id=1, source_target_pairs={{0,64},{8,72},{16,80},{24,88},{32,96},{40,104},{48,112},{56,120},{... | collective-permute-start | bytes 393224 | tf_op jit(solution)/shard_map/ppermute | solution.py:21
  20.2 7.9 %collective-permute-start.8 = (bf16[64,1024]{1,0:T(8,128)(2,1)S(1)}, bf16[64,1024]{1,0:T(8,128)(2,1)S(1)}, u32[]{:S(2)}, u32[]{:S(2)}) collective-permute-start(bf16[64,1024]{1,0:T(8,128)(2,1)S(1)} %get-tuple-element.25.refs_6_), channel_id=1, source_target_pairs={{0,16},{8,24},{16,0},{24,8},{32,48},{40,56},{48,32},{56,40},{64,80... | collective-permute-start | bytes 393224 | tf_op jit(solution)/shard_map/ppermute | solution.py:35
  24.4 22.9 %collective-permute-start.7 = (bf16[256,1024]{1,0:T(8,128)(2,1)S(1)}, bf16[256,1024]{1,0:T(8,128)(2,1)S(1)}, u32[]{:S(2)}, u32[]{:S(2)}) collective-permute-start(bf16[256,1024]{1,0:T(8,128)(2,1)S(1)} %shard_map.103.refs_1_), channel_id=1, source_target_pairs={{0,48},{8,56},{16,0},{24,8},{32,16},{40,24},{48,32},{56,40},{64,11... | collective-permute-start | bytes 1572872 | tf_op jit(solution)/shard_map/ppermute | solution.py:25
  27.5 19.8 %collective-permute-start.6 = (bf16[256,1024]{1,0:T(8,128)(2,1)S(1)}, bf16[256,1024]{1,0:T(8,128)(2,1)S(1)}, u32[]{:S(2)}, u32[]{:S(2)}) collective-permute-start(bf16[256,1024]{1,0:T(8,128)(2,1)S(1)} %shard_map.103.refs_1_), channel_id=1, source_target_pairs={{0,32},{8,40},{16,48},{24,56},{32,0},{40,8},{48,16},{56,24},{64,96... | collective-permute-start | bytes 1572872 | tf_op jit(solution)/shard_map/ppermute | solution.py:25
  28.1 22.9 %collective-permute-start.5 = (bf16[256,1024]{1,0:T(8,128)(2,1)S(1)}, bf16[256,1024]{1,0:T(8,128)(2,1)S(1)}, u32[]{:S(2)}, u32[]{:S(2)}) collective-permute-start(bf16[256,1024]{1,0:T(8,128)(2,1)S(1)} %shard_map.103.refs_1_), channel_id=1, source_target_pairs={{0,16},{8,24},{16,32},{24,40},{32,48},{40,56},{48,0},{56,8},{64,80... | collective-permute-start | bytes 1572872 | tf_op jit(solution)/shard_map/ppermute | solution.py:25
  32.2 6.2 %collective-permute-start.9 = (bf16[64,1024]{1,0:T(8,128)(2,1)S(1)}, bf16[64,1024]{1,0:T(8,128)(2,1)S(1)}, u32[]{:S(2)}, u32[]{:S(2)}) collective-permute-start(bf16[64,1024]{1,0:T(8,128)(2,1)S(1)} %get-tuple-element.25.refs_6_), channel_id=1, source_target_pairs={{0,64},{8,72},{16,80},{24,88},{32,96},{40,104},{48,112},{56,120},{... | collective-permute-start | bytes 393224 | tf_op jit(solution)/shard_map/ppermute | solution.py:31
  38.4 12.6 %collective-permute-start.14 = (bf16[128,896]{1,0:T(8,128)(2,1)S(1)}, bf16[128,896]{1,0:T(8,128)(2,1)S(1)}, u32[]{:S(2)}, u32[]{:S(2)}) collective-permute-start(bf16[128,896]{1,0:T(8,128)(2,1)S(1)} %slice.9), channel_id=1, source_target_pairs={{0,6},{1,7},{2,0},{3,1},{4,2},{5,3},{6,4},{7,5},{8,14},{9,15},{10,... | collective-permute-start | bytes 688136 | tf_op jit(solution)/shard_map/ppermute | solution.py:43
  39.8 11.8 %collective-permute-start.12 = (bf16[128,896]{1,0:T(8,128)(2,1)S(1)}, bf16[128,896]{1,0:T(8,128)(2,1)S(1)}, u32[]{:S(2)}, u32[]{:S(2)}) collective-permute-start(bf16[128,896]{1,0:T(8,128)(2,1)S(1)} %slice.8), channel_id=1, source_target_pairs={{0,2},{1,3},{2,4},{3,5},{4,6},{5,7},{6,0},{7,1},{8,10},{9,11},{10,... | collective-permute-start | bytes 688136 | tf_op jit(solution)/shard_map/ppermute | solution.py:43
  53.8 15.8 %collective-permute-start.20 = (bf16[256,1024]{1,0:T(8,128)(2,1)S(1)}, bf16[256,1024]{1,0:T(8,128)(2,1)S(1)}, u32[]{:S(2)}, u32[]{:S(2)}) collective-permute-start(bf16[256,1024]{1,0:T(8,128)(2,1)S(1)} %get-tuple-element.33.refs_6_.refs_3_), channel_id=1, source_target_pairs={{0,32},{8,40},{16,48},{24,56},{32,0},{40,8},{48,16},{56,24},{64,96... | collective-permute-start | bytes 1572872 | tf_op jit(solution)/shard_map/ppermute | solution.py:35
  57.9 11.7 %collective-permute-start.19 = (bf16[1024,896]{1,0:T(8,128)(2,1)S(1)}, bf16[1024,896]{1,0:T(8,128)(2,1)S(1)}, u32[]{:S(2)}, u32[]{:S(2)}) collective-permute-start(bf16[1024,896]{1,0:T(8,128)(2,1)S(1)} %shard_map.107.refs_1_), channel_id=1, source_target_pairs={{0,1},{1,0},{2,3},{3,2},{4,5},{5,4},{6,7},{7,6},{8,9},{9,8},{10,11... | collective-permute-start | bytes 5505032 | tf_op jit(solution)/shard_map/ppermute | solution.py:47
  60.6 16.9 %collective-permute-start.16 = (bf16[128,896]{1,0:T(8,128)(2,1)S(1)}, bf16[128,896]{1,0:T(8,128)(2,1)S(1)}, u32[]{:S(2)}, u32[]{:S(2)}) collective-permute-start(bf16[128,896]{1,0:T(8,128)(2,1)S(1)} %get-tuple-element.30), channel_id=1, source_target_pairs={{0,2},{1,3},{2,4},{3,5},{4,6},{5,7},{6,0},{7,1},{8,10},{9,11},{10,... | collective-permute-start | bytes 688136 | tf_op jit(solution)/shard_map/ppermute | solution.py:43
  63.0 23.9 %collective-permute-start.17 = (bf16[128,896]{1,0:T(8,128)(2,1)S(1)}, bf16[128,896]{1,0:T(8,128)(2,1)S(1)}, u32[]{:S(2)}, u32[]{:S(2)}) collective-permute-start(bf16[128,896]{1,0:T(8,128)(2,1)S(1)} %get-tuple-element.31), channel_id=1, source_target_pairs={{0,4},{1,5},{2,6},{3,7},{4,0},{5,1},{6,2},{7,3},{8,12},{9,13},{10,... | collective-permute-start | bytes 688136 | tf_op jit(solution)/shard_map/ppermute | solution.py:43
  66.2 21.3 %collective-permute-start.18 = (bf16[128,896]{1,0:T(8,128)(2,1)S(1)}, bf16[128,896]{1,0:T(8,128)(2,1)S(1)}, u32[]{:S(2)}, u32[]{:S(2)}) collective-permute-start(bf16[128,896]{1,0:T(8,128)(2,1)S(1)} %get-tuple-element.32), channel_id=1, source_target_pairs={{0,6},{1,7},{2,0},{3,1},{4,2},{5,3},{6,4},{7,5},{8,14},{9,15},{10,... | collective-permute-start | bytes 688136 | tf_op jit(solution)/shard_map/ppermute | solution.py:43
  74.5 38.6 %collective-permute-start.28 = (bf16[512,1024]{1,0:T(8,128)(2,1)S(1)}, bf16[512,1024]{1,0:T(8,128)(2,1)S(1)}, u32[]{:S(2)}, u32[]{:S(2)}) collective-permute-start(bf16[512,1024]{1,0:T(8,128)(2,1)S(1)} %get-tuple-element.37.refs_1_), channel_id=1, source_target_pairs={{0,128},{8,136},{16,144},{24,152},{32,160},{40,168},{48,176},{56,1... | collective-permute-start | bytes 3145736 | tf_op jit(solution)/shard_map/ppermute | solution.py:31
  88.1 10.4 %collective-permute-start.23 = (bf16[128,896]{1,0:T(8,128)(2,1)S(1)}, bf16[128,896]{1,0:T(8,128)(2,1)S(1)}, u32[]{:S(2)}, u32[]{:S(2)}) collective-permute-start(bf16[128,896]{1,0:T(8,128)(2,1)S(1)} %shard_map.109.refs_1_), channel_id=1, source_target_pairs={{0,2},{1,3},{2,4},{3,5},{4,6},{5,7},{6,0},{7,1},{8,10},{9,11},{10,... | collective-permute-start | bytes 688136 | tf_op jit(solution)/shard_map/ppermute | solution.py:43
  91.0 20.1 %collective-permute-start.22 = (bf16[128,896]{1,0:T(8,128)(2,1)S(1)}, bf16[128,896]{1,0:T(8,128)(2,1)S(1)}, u32[]{:S(2)}, u32[]{:S(2)}) collective-permute-start(bf16[128,896]{1,0:T(8,128)(2,1)S(1)} %shard_map.109.refs_1_), channel_id=1, source_target_pairs={{0,4},{1,5},{2,6},{3,7},{4,0},{5,1},{6,2},{7,3},{8,12},{9,13},{10,... | collective-permute-start | bytes 688136 | tf_op jit(solution)/shard_map/ppermute | solution.py:43
  93.1 18.5 %collective-permute-start.21 = (bf16[128,896]{1,0:T(8,128)(2,1)S(1)}, bf16[128,896]{1,0:T(8,128)(2,1)S(1)}, u32[]{:S(2)}, u32[]{:S(2)}) collective-permute-start(bf16[128,896]{1,0:T(8,128)(2,1)S(1)} %shard_map.109.refs_1_), channel_id=1, source_target_pairs={{0,6},{1,7},{2,0},{3,1},{4,2},{5,3},{6,4},{7,5},{8,14},{9,15},{10,... | collective-permute-start | bytes 688136 | tf_op jit(solution)/shard_map/ppermute | solution.py:43
  94.9 16.7 %collective-permute-start.24 = (bf16[128,896]{1,0:T(8,128)(2,1)S(1)}, bf16[128,896]{1,0:T(8,128)(2,1)S(1)}, u32[]{:S(2)}, u32[]{:S(2)}) collective-permute-start(bf16[128,896]{1,0:T(8,128)(2,1)S(1)} %shard_map.109.refs_1_), channel_id=1, source_target_pairs={{0,1},{1,0},{2,3},{3,2},{4,5},{5,4},{6,7},{7,6},{8,9},{9,8},{10,11... | collective-permute-start | bytes 688136 | tf_op jit(solution)/shard_map/ppermute | solution.py:47
  98.5 13.1 %collective-permute-start.27 = (bf16[128,896]{1,0:T(8,128)(2,1)S(1)}, bf16[128,896]{1,0:T(8,128)(2,1)S(1)}, u32[]{:S(2)}, u32[]{:S(2)}) collective-permute-start(bf16[128,896]{1,0:T(8,128)(2,1)S(1)} %collective-permute-done.23.refs_4_), channel_id=1, source_target_pairs={{0,1},{1,0},{2,3},{3,2},{4,5},{5,4},{6,7},{7,6},{8,9},{9,8},{10,11... | collective-permute-start | bytes 688136 | tf_op jit(solution)/shard_map/ppermute | solution.py:47
  119.4 37.5 %all-to-all-start = ((bf16[32,32,1024]{2,1,0:T(8,128)(2,1)}), bf16[32,32,1024]{2,1,0:T(8,128)(2,1)S(1)}, u32[]{:S(2)}, u32[]{:S(2)}) async-start(bf16[32,32,1024]{2,1,0:T(8,128)(2,1)} %bitcast.6), calls=%async_computation | async-start | bytes 4194304 | tf_op jit(solution)/shard_map/all_to_all | solution.py:311
  (13 other events, 137.4 us)

commit v4 on v2

--- a/solution.py
+++ b/solution.py
@@ -178,10 +178,13 @@
 
 
 def sum_kernel(pos, parts, out):
-    total = parts[0].astype(F32)
-    for i in range(1, 32):
-        total = total + parts[i].astype(F32)
-    out[...] = total.astype(BF)
+    for start in range(0, DB, 256):
+        cols = slice(start, start + 256)
+        even, odd = parts[0, :, cols].astype(F32), parts[1, :, cols].astype(F32)
+        for i in range(2, 32, 2):
+            even = even + parts[i, :, cols].astype(F32)
+            odd = odd + parts[i + 1, :, cols].astype(F32)
+        out[:, cols] = (even + odd).astype(BF)
 
 
 def input_grad_kernel(pos, *refs):

time: 160 us -> 160 us (level)
  no operation moved by 1% of the time
where the time goes in v4:
time: 160 us; the launch traced here: 159 us
  waiting for transfers between devices  78.3 us (49%)
  starting transfers between devices  48.3 us (30%)
  Pallas kernels  27.1 us (17%)
  local copies, waits for them, and re-layouts  4.35 us (3%)
    ppermute x10, waiting for transfers between devices, shift_zh(): lax.ppermute(value, 'wid', [(w, (w + 2 * step) % 8) for w in range(8)])  28.6 us
    pallas_call x10, Pallas kernels, run(): pl.pallas_call(body, out_shape=[(pltpu.HBM if o[2:] else jax.ShapeDtypeSt...  27.1 us
    all_to_all x1, waiting for transfers between devices, per_device(): lax.all_to_all(partial, 'hid', split_axis=0, concat_axis=0, tiled=True)  21 us
    ppermute x10, starting transfers between devices, shift_zh(): lax.ppermute(value, 'wid', [(w, (w + 2 * step) % 8) for w in range(8)])  20.2 us
    ppermute x3, waiting for transfers between devices, shift_y(): lax.ppermute(value, 'hid', [(h, h // 8 * 8 + (h % 8 + 2 * step) % 8) for...  8.41 us
    all_to_all x1, starting transfers between devices, per_device(): lax.all_to_all(partial, 'hid', split_axis=0, concat_axis=0, tiled=True)  6.46 us
    ppermute x3, waiting for transfers between devices, swap_x(): return lax.ppermute(value, 'hid', [(h, h ^ 8 * bit) for h in range(32)])  5.53 us
    ppermute x3, starting transfers between devices, swap_x(): return lax.ppermute(value, 'hid', [(h, h ^ 8 * bit) for h in range(32)])  5.05 us
  transfers between devices with their start and end apart: 30, of which 20 were waited for; matrix products, arithmetic and copies ran while one was open for 0% of the time, Pallas kernels for 9%

profile of v4, /device:TPU:64, one launch (start us, length us, event | category | flops | bytes accessed | tf_op | source)
XLA Modules:
  0.0 158.9 jit_solution(6274063017622660583)
XLA Ops:
  2.8 2.6 %collective-permute-done.1.refs_2_ = bf16[32,1024]{1,0:T(8,128)(2,1)S(1)} collective-permute-done((bf16[32,1024]{1,0:T(8,128)(2,1)}, bf16[32,1024]{1,0:T(8,128)(2,1)S(1)}, u32[]{:S(2)}, u32[]{:S(2)}) %collective-permute-start.1) | collective-permute-done | bytes 65568 | tf_op jit(solution)/shard_map/ppermute | solution.py:39
  9.2 4.0 %collective-permute-start.11 = (bf16[256,896]{1,0:T(8,128)(2,1)S(1)}, bf16[256,896]{1,0:T(8,128)(2,1)S(1)}, u32[]{:S(2)}, u32[]{:S(2)}) collective-permute-start(bf16[256,896]{1,0:T(8,128)(2,1)S(1)} %get-tuple-element.26.refs_1_), channel_id=1, source_target_pairs={{0,2},{1,3},{2,4},{3,5},{4,6},{5,7},{6,0},{7,1},{8,10},{9,11},{10,... | collective-permute-start | bytes 1376264 | tf_op jit(solution)/shard_map/ppermute | solution.py:43
  13.2 2.8 %collective-permute-start.4 = (bf16[64,1024]{1,0:T(8,128)(2,1)S(1)}, bf16[64,1024]{1,0:T(8,128)(2,1)S(1)}, u32[]{:S(2)}, u32[]{:S(2)}) collective-permute-start(bf16[64,1024]{1,0:T(8,128)(2,1)S(1)} %get-tuple-element.24.refs_1_), channel_id=1, source_target_pairs={{0,192},{8,200},{16,208},{24,216},{32,224},{40,232},{48,240},{56,2... | collective-permute-start | bytes 393224 | tf_op jit(solution)/shard_map/ppermute | solution.py:21
  17.6 2.5 %collective-permute-done.4.refs_4_ = bf16[64,1024]{1,0:T(8,128)(2,1)S(1)} collective-permute-done((bf16[64,1024]{1,0:T(8,128)(2,1)S(1)}, bf16[64,1024]{1,0:T(8,128)(2,1)S(1)}, u32[]{:S(2)}, u32[]{:S(2)}) %collective-permute-start.4) | collective-permute-done | bytes 131104 | tf_op jit(solution)/shard_map/ppermute | solution.py:21
  24.4 3.1 %collective-permute-start.7 = (bf16[256,1024]{1,0:T(8,128)(2,1)S(1)}, bf16[256,1024]{1,0:T(8,128)(2,1)S(1)}, u32[]{:S(2)}, u32[]{:S(2)}) collective-permute-start(bf16[256,1024]{1,0:T(8,128)(2,1)S(1)} %shard_map.103.refs_1_), channel_id=1, source_target_pairs={{0,48},{8,56},{16,0},{24,8},{32,16},{40,24},{48,32},{56,40},{64,11... | collective-permute-start | bytes 1572872 | tf_op jit(solution)/shard_map/ppermute | solution.py:25
  29.1 3.1 %collective-permute-done.13.refs_2_ = bf16[256,896]{1,0:T(8,128)(2,1)S(1)} collective-permute-done((bf16[256,896]{1,0:T(8,128)(2,1)S(1)}, bf16[256,896]{1,0:T(8,128)(2,1)S(1)}, u32[]{:S(2)}, u32[]{:S(2)}) %collective-permute-start.13) | collective-permute-done | bytes 458784 | tf_op jit(solution)/shard_map/ppermute | solution.py:43
  34.3 4.1 %collective-permute-done.9.refs_8_ = bf16[64,1024]{1,0:T(8,128)(2,1)S(1)} collective-permute-done((bf16[64,1024]{1,0:T(8,128)(2,1)S(1)}, bf16[64,1024]{1,0:T(8,128)(2,1)S(1)}, u32[]{:S(2)}, u32[]{:S(2)}) %collective-permute-start.9) | collective-permute-done | bytes 131104 | tf_op jit(solution)/shard_map/ppermute | solution.py:31
  39.8 2.7 %collective-permute-start.12 = (bf16[128,896]{1,0:T(8,128)(2,1)S(1)}, bf16[128,896]{1,0:T(8,128)(2,1)S(1)}, u32[]{:S(2)}, u32[]{:S(2)}) collective-permute-start(bf16[128,896]{1,0:T(8,128)(2,1)S(1)} %slice.8), channel_id=1, source_target_pairs={{0,2},{1,3},{2,4},{3,5},{4,6},{5,7},{6,0},{7,1},{8,10},{9,11},{10,... | collective-permute-start | bytes 688136 | tf_op jit(solution)/shard_map/ppermute | solution.py:43
  42.6 4.7 %collective-permute-done.7.refs_4_ = bf16[256,1024]{1,0:T(8,128)(2,1)S(1)} collective-permute-done((bf16[256,1024]{1,0:T(8,128)(2,1)S(1)}, bf16[256,1024]{1,0:T(8,128)(2,1)S(1)}, u32[]{:S(2)}, u32[]{:S(2)}) %collective-permute-start.7) | collective-permute-done | bytes 524320 | tf_op jit(solution)/shard_map/ppermute | solution.py:25
  47.3 3.7 %collective-permute-done.5.refs_2_ = bf16[256,1024]{1,0:T(8,128)(2,1)S(1)} collective-permute-done((bf16[256,1024]{1,0:T(8,128)(2,1)S(1)}, bf16[256,1024]{1,0:T(8,128)(2,1)S(1)}, u32[]{:S(2)}, u32[]{:S(2)}) %collective-permute-start.5) | collective-permute-done | bytes 524320 | tf_op jit(solution)/shard_map/ppermute | solution.py:25
  51.7 3.0 %shard_map.104 = (bf16[1024,1024]{1,0:T(8,128)(2,1)S(1)}, f32[512,896]{1,0:T(8,128)S(1)}, f32[512,896]{1,0:T(8,128)S(1)}, bf16[256,1024]{1,0:T(8,128)(2,1)S(1)}) custom-call(s32[5]{0:T(128)S(1)} %stack.23.refs_0_, bf16[256,1024]{1,0:T(8,128)(2,1)S(1)} %shard_map.103.refs_1_, bf16[256,1024]{1,0:T(8,128)(2,1)S(1)} %collective-permute-done.5.refs_2_, ...), custom_call_target="tpu_custom_call" | custom-call | flops 22548578304 | bytes 83886080 | tf_op jit(solution)/shard_map/pallas_call | solution.py:83
  54.8 3.5 %collective-permute-start.20 = (bf16[256,1024]{1,0:T(8,128)(2,1)S(1)}, bf16[256,1024]{1,0:T(8,128)(2,1)S(1)}, u32[]{:S(2)}, u32[]{:S(2)}) collective-permute-start(bf16[256,1024]{1,0:T(8,128)(2,1)S(1)} %get-tuple-element.33.refs_6_.refs_3_), channel_id=1, source_target_pairs={{0,32},{8,40},{16,48},{24,56},{32,0},{40,8},{48,16},{56,24},{64,96... | collective-permute-start | bytes 1572872 | tf_op jit(solution)/shard_map/ppermute | solution.py:35
  62.2 3.1 %collective-permute-start.17 = (bf16[128,896]{1,0:T(8,128)(2,1)S(1)}, bf16[128,896]{1,0:T(8,128)(2,1)S(1)}, u32[]{:S(2)}, u32[]{:S(2)}) collective-permute-start(bf16[128,896]{1,0:T(8,128)(2,1)S(1)} %get-tuple-element.31), channel_id=1, source_target_pairs={{0,4},{1,5},{2,6},{3,7},{4,0},{5,1},{6,2},{7,3},{8,12},{9,13},{10,... | collective-permute-start | bytes 688136 | tf_op jit(solution)/shard_map/ppermute | solution.py:43
  66.3 4.3 %collective-permute-done.20.refs_4_ = bf16[256,1024]{1,0:T(8,128)(2,1)S(1)} collective-permute-done((bf16[256,1024]{1,0:T(8,128)(2,1)S(1)}, bf16[256,1024]{1,0:T(8,128)(2,1)S(1)}, u32[]{:S(2)}, u32[]{:S(2)}) %collective-permute-start.20) | collective-permute-done | bytes 524320 | tf_op jit(solution)/shard_map/ppermute | solution.py:35
  70.7 4.9 %shard_map.107 = (bf16[896,1024]{1,0:T(8,128)(2,1)}, f32[1024,896]{1,0:T(8,128)S(1)}, f32[1024,896]{1,0:T(8,128)S(1)}, bf16[512,1024]{1,0:T(8,128)(2,1)S(1)}) custom-call(s32[5]{0:T(128)S(1)} %stack.23.refs_0_, bf16[1024,896]{1,0:T(8,128)(2,1)S(1)} %shard_map.106.refs_1_, bf16[1024,896]{1,0:T(8,128)(2,1)S(1)} %collective-permute-done.19.refs_2_, ...), custom_call_target="tpu_custom_call" | custom-call | flops 1879048192 | bytes 16777216 | tf_op jit(solution)/shard_map/pallas_call | solution.py:83
  75.6 3.0 %collective-permute-start.28 = (bf16[512,1024]{1,0:T(8,128)(2,1)S(1)}, bf16[512,1024]{1,0:T(8,128)(2,1)S(1)}, u32[]{:S(2)}, u32[]{:S(2)}) collective-permute-start(bf16[512,1024]{1,0:T(8,128)(2,1)S(1)} %get-tuple-element.37.refs_1_), channel_id=1, source_target_pairs={{0,128},{8,136},{16,144},{24,152},{32,160},{40,168},{48,176},{56,1... | collective-permute-start | bytes 3145736 | tf_op jit(solution)/shard_map/ppermute | solution.py:31
  78.6 7.1 %collective-permute-done.17.refs_3_ = bf16[128,896]{1,0:T(8,128)(2,1)S(1)} collective-permute-done((bf16[128,896]{1,0:T(8,128)(2,1)S(1)}, bf16[128,896]{1,0:T(8,128)(2,1)S(1)}, u32[]{:S(2)}, u32[]{:S(2)}) %collective-permute-start.17) | collective-permute-done | bytes 229408 | tf_op jit(solution)/shard_map/ppermute | solution.py:43
  87.4 2.8 %collective-permute-start.23 = (bf16[128,896]{1,0:T(8,128)(2,1)S(1)}, bf16[128,896]{1,0:T(8,128)(2,1)S(1)}, u32[]{:S(2)}, u32[]{:S(2)}) collective-permute-start(bf16[128,896]{1,0:T(8,128)(2,1)S(1)} %shard_map.108.refs_1_), channel_id=1, source_target_pairs={{0,2},{1,3},{2,4},{3,5},{4,6},{5,7},{6,0},{7,1},{8,10},{9,11},{10,... | collective-permute-start | bytes 688136 | tf_op jit(solution)/shard_map/ppermute | solution.py:43
  94.1 3.7 %collective-permute-done.23.refs_4_ = bf16[128,896]{1,0:T(8,128)(2,1)S(1)} collective-permute-done((bf16[128,896]{1,0:T(8,128)(2,1)S(1)}, bf16[128,896]{1,0:T(8,128)(2,1)S(1)}, u32[]{:S(2)}, u32[]{:S(2)}) %collective-permute-start.23) | collective-permute-done | bytes 229408 | tf_op jit(solution)/shard_map/ppermute | solution.py:43
  97.8 12.5 %collective-permute-done.22.refs_3_ = bf16[128,896]{1,0:T(8,128)(2,1)S(1)} collective-permute-done((bf16[128,896]{1,0:T(8,128)(2,1)S(1)}, bf16[128,896]{1,0:T(8,128)(2,1)S(1)}, u32[]{:S(2)}, u32[]{:S(2)}) %collective-permute-start.22) | collective-permute-done | bytes 229408 | tf_op jit(solution)/shard_map/ppermute | solution.py:43
  112.3 6.2 %shard_map.109 = (bf16[1024,1024]{1,0:T(8,128)(2,1)}, bf16[1024,896]{1,0:T(8,128)(2,1)}, bf16[1024,896]{1,0:T(8,128)(2,1)}) custom-call(s32[5]{0:T(128)S(1)} %stack.23.refs_0_, bf16[128,896]{1,0:T(8,128)(2,1)S(1)} %shard_map.108.refs_1_, bf16[128,896]{1,0:T(8,128)(2,1)S(1)} %collective-permute-done.21.refs_2_, ...), custom_call_target="tpu_custom_call" | custom-call | flops 3758096384 | bytes 15728640 | tf_op jit(solution)/shard_map/pallas_call | solution.py:83
  118.6 6.5 %all-to-all-start = ((bf16[32,32,1024]{2,1,0:T(8,128)(2,1)}), bf16[32,32,1024]{2,1,0:T(8,128)(2,1)S(1)}, u32[]{:S(2)}, u32[]{:S(2)}) async-start(bf16[32,32,1024]{2,1,0:T(8,128)(2,1)} %bitcast.6), calls=%async_computation | async-start | bytes 4194304 | tf_op jit(solution)/shard_map/all_to_all | solution.py:303
  129.3 7.1 %shard_map.111 = (bf16[1024,896]{1,0:T(8,128)(2,1)}, bf16[1024,896]{1,0:T(8,128)(2,1)}) custom-call(s32[5]{0:T(128)S(1)} %stack.23.refs_0_, bf16[512,1024]{1,0:T(8,128)(2,1)S(1)} %get-tuple-element.37.refs_1_, bf16[512,1024]{1,0:T(8,128)(2,1)S(1)} %copy-done.4, bf16[1024,896]{1,0:T(8,128)(2,1)S(1)} %copy-done.5, bf16[1024,896]{1,0:T(8,128)(2,1)S(1)} %copy-done.6), custom_call_target="tpu_custom_call" | custom-call | flops 3758096384 | bytes 10485760 | tf_op jit(solution)/shard_map/pallas_call | solution.py:83
  136.4 21.0 %all-to-all-done.refs_1_ = bf16[32,32,1024]{2,1,0:T(8,128)(2,1)S(1)} async-done(((bf16[32,32,1024]{2,1,0:T(8,128)(2,1)}), bf16[32,32,1024]{2,1,0:T(8,128)(2,1)S(1)}, u32[]{:S(2)}, u32[]{:S(2)}) %all-to-all-start) | async-done | bytes 2097184 | tf_op jit(solution)/shard_map/all_to_all | solution.py:303
  (63 shorter events, 35.8 us)
Async XLA Ops:
  9.0 23.3 %collective-permute-start.13 = (bf16[256,896]{1,0:T(8,128)(2,1)S(1)}, bf16[256,896]{1,0:T(8,128)(2,1)S(1)}, u32[]{:S(2)}, u32[]{:S(2)}) collective-permute-start(bf16[256,896]{1,0:T(8,128)(2,1)S(1)} %get-tuple-element.26.refs_1_), channel_id=1, source_target_pairs={{0,6},{1,7},{2,0},{3,1},{4,2},{5,3},{6,4},{7,5},{8,14},{9,15},{10,... | collective-permute-start | bytes 1376264 | tf_op jit(solution)/shard_map/ppermute | solution.py:43
  9.2 24.5 %collective-permute-start.11 = (bf16[256,896]{1,0:T(8,128)(2,1)S(1)}, bf16[256,896]{1,0:T(8,128)(2,1)S(1)}, u32[]{:S(2)}, u32[]{:S(2)}) collective-permute-start(bf16[256,896]{1,0:T(8,128)(2,1)S(1)} %get-tuple-element.26.refs_1_), channel_id=1, source_target_pairs={{0,2},{1,3},{2,4},{3,5},{4,6},{5,7},{6,0},{7,1},{8,10},{9,11},{10,... | collective-permute-start | bytes 1376264 | tf_op jit(solution)/shard_map/ppermute | solution.py:43
  13.2 7.0 %collective-permute-start.4 = (bf16[64,1024]{1,0:T(8,128)(2,1)S(1)}, bf16[64,1024]{1,0:T(8,128)(2,1)S(1)}, u32[]{:S(2)}, u32[]{:S(2)}) collective-permute-start(bf16[64,1024]{1,0:T(8,128)(2,1)S(1)} %get-tuple-element.24.refs_1_), channel_id=1, source_target_pairs={{0,192},{8,200},{16,208},{24,216},{32,224},{40,232},{48,240},{56,2... | collective-permute-start | bytes 393224 | tf_op jit(solution)/shard_map/ppermute | solution.py:21
  15.9 6.6 %collective-permute-start.3 = (bf16[64,1024]{1,0:T(8,128)(2,1)S(1)}, bf16[64,1024]{1,0:T(8,128)(2,1)S(1)}, u32[]{:S(2)}, u32[]{:S(2)}) collective-permute-start(bf16[64,1024]{1,0:T(8,128)(2,1)S(1)} %get-tuple-element.24.refs_1_), channel_id=1, source_target_pairs={{0,128},{8,136},{16,144},{24,152},{32,160},{40,168},{48,176},{56,1... | collective-permute-start | bytes 393224 | tf_op jit(solution)/shard_map/ppermute | solution.py:21
  16.7 7.1 %collective-permute-start.2 = (bf16[64,1024]{1,0:T(8,128)(2,1)S(1)}, bf16[64,1024]{1,0:T(8,128)(2,1)S(1)}, u32[]{:S(2)}, u32[]{:S(2)}) collective-permute-start(bf16[64,1024]{1,0:T(8,128)(2,1)S(1)} %get-tuple-element.24.refs_1_), channel_id=1, source_target_pairs={{0,64},{8,72},{16,80},{24,88},{32,96},{40,104},{48,112},{56,120},{... | collective-permute-start | bytes 393224 | tf_op jit(solution)/shard_map/ppermute | solution.py:21
  20.2 7.9 %collective-permute-start.8 = (bf16[64,1024]{1,0:T(8,128)(2,1)S(1)}, bf16[64,1024]{1,0:T(8,128)(2,1)S(1)}, u32[]{:S(2)}, u32[]{:S(2)}) collective-permute-start(bf16[64,1024]{1,0:T(8,128)(2,1)S(1)} %get-tuple-element.25.refs_6_), channel_id=1, source_target_pairs={{0,16},{8,24},{16,0},{24,8},{32,48},{40,56},{48,32},{56,40},{64,80... | collective-permute-start | bytes 393224 | tf_op jit(solution)/shard_map/ppermute | solution.py:35
  24.4 22.9 %collective-permute-start.7 = (bf16[256,1024]{1,0:T(8,128)(2,1)S(1)}, bf16[256,1024]{1,0:T(8,128)(2,1)S(1)}, u32[]{:S(2)}, u32[]{:S(2)}) collective-permute-start(bf16[256,1024]{1,0:T(8,128)(2,1)S(1)} %shard_map.103.refs_1_), channel_id=1, source_target_pairs={{0,48},{8,56},{16,0},{24,8},{32,16},{40,24},{48,32},{56,40},{64,11... | collective-permute-start | bytes 1572872 | tf_op jit(solution)/shard_map/ppermute | solution.py:25
  27.5 19.8 %collective-permute-start.6 = (bf16[256,1024]{1,0:T(8,128)(2,1)S(1)}, bf16[256,1024]{1,0:T(8,128)(2,1)S(1)}, u32[]{:S(2)}, u32[]{:S(2)}) collective-permute-start(bf16[256,1024]{1,0:T(8,128)(2,1)S(1)} %shard_map.103.refs_1_), channel_id=1, source_target_pairs={{0,32},{8,40},{16,48},{24,56},{32,0},{40,8},{48,16},{56,24},{64,96... | collective-permute-start | bytes 1572872 | tf_op jit(solution)/shard_map/ppermute | solution.py:25
  28.1 22.9 %collective-permute-start.5 = (bf16[256,1024]{1,0:T(8,128)(2,1)S(1)}, bf16[256,1024]{1,0:T(8,128)(2,1)S(1)}, u32[]{:S(2)}, u32[]{:S(2)}) collective-permute-start(bf16[256,1024]{1,0:T(8,128)(2,1)S(1)} %shard_map.103.refs_1_), channel_id=1, source_target_pairs={{0,16},{8,24},{16,32},{24,40},{32,48},{40,56},{48,0},{56,8},{64,80... | collective-permute-start | bytes 1572872 | tf_op jit(solution)/shard_map/ppermute | solution.py:25
  32.2 6.2 %collective-permute-start.9 = (bf16[64,1024]{1,0:T(8,128)(2,1)S(1)}, bf16[64,1024]{1,0:T(8,128)(2,1)S(1)}, u32[]{:S(2)}, u32[]{:S(2)}) collective-permute-start(bf16[64,1024]{1,0:T(8,128)(2,1)S(1)} %get-tuple-element.25.refs_6_), channel_id=1, source_target_pairs={{0,64},{8,72},{16,80},{24,88},{32,96},{40,104},{48,112},{56,120},{... | collective-permute-start | bytes 393224 | tf_op jit(solution)/shard_map/ppermute | solution.py:31
  38.4 12.6 %collective-permute-start.14 = (bf16[128,896]{1,0:T(8,128)(2,1)S(1)}, bf16[128,896]{1,0:T(8,128)(2,1)S(1)}, u32[]{:S(2)}, u32[]{:S(2)}) collective-permute-start(bf16[128,896]{1,0:T(8,128)(2,1)S(1)} %slice.9), channel_id=1, source_target_pairs={{0,6},{1,7},{2,0},{3,1},{4,2},{5,3},{6,4},{7,5},{8,14},{9,15},{10,... | collective-permute-start | bytes 688136 | tf_op jit(solution)/shard_map/ppermute | solution.py:43
  39.8 11.8 %collective-permute-start.12 = (bf16[128,896]{1,0:T(8,128)(2,1)S(1)}, bf16[128,896]{1,0:T(8,128)(2,1)S(1)}, u32[]{:S(2)}, u32[]{:S(2)}) collective-permute-start(bf16[128,896]{1,0:T(8,128)(2,1)S(1)} %slice.8), channel_id=1, source_target_pairs={{0,2},{1,3},{2,4},{3,5},{4,6},{5,7},{6,0},{7,1},{8,10},{9,11},{10,... | collective-permute-start | bytes 688136 | tf_op jit(solution)/shard_map/ppermute | solution.py:43
  54.8 15.8 %collective-permute-start.20 = (bf16[256,1024]{1,0:T(8,128)(2,1)S(1)}, bf16[256,1024]{1,0:T(8,128)(2,1)S(1)}, u32[]{:S(2)}, u32[]{:S(2)}) collective-permute-start(bf16[256,1024]{1,0:T(8,128)(2,1)S(1)} %get-tuple-element.33.refs_6_.refs_3_), channel_id=1, source_target_pairs={{0,32},{8,40},{16,48},{24,56},{32,0},{40,8},{48,16},{56,24},{64,96... | collective-permute-start | bytes 1572872 | tf_op jit(solution)/shard_map/ppermute | solution.py:35
  59.0 11.7 %collective-permute-start.19 = (bf16[1024,896]{1,0:T(8,128)(2,1)S(1)}, bf16[1024,896]{1,0:T(8,128)(2,1)S(1)}, u32[]{:S(2)}, u32[]{:S(2)}) collective-permute-start(bf16[1024,896]{1,0:T(8,128)(2,1)S(1)} %shard_map.106.refs_1_), channel_id=1, source_target_pairs={{0,1},{1,0},{2,3},{3,2},{4,5},{5,4},{6,7},{7,6},{8,9},{9,8},{10,11... | collective-permute-start | bytes 5505032 | tf_op jit(solution)/shard_map/ppermute | solution.py:47
  59.8 18.8 %collective-permute-start.16 = (bf16[128,896]{1,0:T(8,128)(2,1)S(1)}, bf16[128,896]{1,0:T(8,128)(2,1)S(1)}, u32[]{:S(2)}, u32[]{:S(2)}) collective-permute-start(bf16[128,896]{1,0:T(8,128)(2,1)S(1)} %get-tuple-element.30), channel_id=1, source_target_pairs={{0,2},{1,3},{2,4},{3,5},{4,6},{5,7},{6,0},{7,1},{8,10},{9,11},{10,... | collective-permute-start | bytes 688136 | tf_op jit(solution)/shard_map/ppermute | solution.py:43
  62.2 23.4 %collective-permute-start.17 = (bf16[128,896]{1,0:T(8,128)(2,1)S(1)}, bf16[128,896]{1,0:T(8,128)(2,1)S(1)}, u32[]{:S(2)}, u32[]{:S(2)}) collective-permute-start(bf16[128,896]{1,0:T(8,128)(2,1)S(1)} %get-tuple-element.31), channel_id=1, source_target_pairs={{0,4},{1,5},{2,6},{3,7},{4,0},{5,1},{6,2},{7,3},{8,12},{9,13},{10,... | collective-permute-start | bytes 688136 | tf_op jit(solution)/shard_map/ppermute | solution.py:43
  65.4 21.3 %collective-permute-start.18 = (bf16[128,896]{1,0:T(8,128)(2,1)S(1)}, bf16[128,896]{1,0:T(8,128)(2,1)S(1)}, u32[]{:S(2)}, u32[]{:S(2)}) collective-permute-start(bf16[128,896]{1,0:T(8,128)(2,1)S(1)} %get-tuple-element.32), channel_id=1, source_target_pairs={{0,6},{1,7},{2,0},{3,1},{4,2},{5,3},{6,4},{7,5},{8,14},{9,15},{10,... | collective-permute-start | bytes 688136 | tf_op jit(solution)/shard_map/ppermute | solution.py:43
  75.6 36.8 %collective-permute-start.28 = (bf16[512,1024]{1,0:T(8,128)(2,1)S(1)}, bf16[512,1024]{1,0:T(8,128)(2,1)S(1)}, u32[]{:S(2)}, u32[]{:S(2)}) collective-permute-start(bf16[512,1024]{1,0:T(8,128)(2,1)S(1)} %get-tuple-element.37.refs_1_), channel_id=1, source_target_pairs={{0,128},{8,136},{16,144},{24,152},{32,160},{40,168},{48,176},{56,1... | collective-permute-start | bytes 3145736 | tf_op jit(solution)/shard_map/ppermute | solution.py:31
  87.4 10.4 %collective-permute-start.23 = (bf16[128,896]{1,0:T(8,128)(2,1)S(1)}, bf16[128,896]{1,0:T(8,128)(2,1)S(1)}, u32[]{:S(2)}, u32[]{:S(2)}) collective-permute-start(bf16[128,896]{1,0:T(8,128)(2,1)S(1)} %shard_map.108.refs_1_), channel_id=1, source_target_pairs={{0,2},{1,3},{2,4},{3,5},{4,6},{5,7},{6,0},{7,1},{8,10},{9,11},{10,... | collective-permute-start | bytes 688136 | tf_op jit(solution)/shard_map/ppermute | solution.py:43
  90.2 20.1 %collective-permute-start.22 = (bf16[128,896]{1,0:T(8,128)(2,1)S(1)}, bf16[128,896]{1,0:T(8,128)(2,1)S(1)}, u32[]{:S(2)}, u32[]{:S(2)}) collective-permute-start(bf16[128,896]{1,0:T(8,128)(2,1)S(1)} %shard_map.108.refs_1_), channel_id=1, source_target_pairs={{0,4},{1,5},{2,6},{3,7},{4,0},{5,1},{6,2},{7,3},{8,12},{9,13},{10,... | collective-permute-start | bytes 688136 | tf_op jit(solution)/shard_map/ppermute | solution.py:43
  92.4 18.5 %collective-permute-start.21 = (bf16[128,896]{1,0:T(8,128)(2,1)S(1)}, bf16[128,896]{1,0:T(8,128)(2,1)S(1)}, u32[]{:S(2)}, u32[]{:S(2)}) collective-permute-start(bf16[128,896]{1,0:T(8,128)(2,1)S(1)} %shard_map.108.refs_1_), channel_id=1, source_target_pairs={{0,6},{1,7},{2,0},{3,1},{4,2},{5,3},{6,4},{7,5},{8,14},{9,15},{10,... | collective-permute-start | bytes 688136 | tf_op jit(solution)/shard_map/ppermute | solution.py:43
  94.1 16.7 %collective-permute-start.24 = (bf16[128,896]{1,0:T(8,128)(2,1)S(1)}, bf16[128,896]{1,0:T(8,128)(2,1)S(1)}, u32[]{:S(2)}, u32[]{:S(2)}) collective-permute-start(bf16[128,896]{1,0:T(8,128)(2,1)S(1)} %shard_map.108.refs_1_), channel_id=1, source_target_pairs={{0,1},{1,0},{2,3},{3,2},{4,5},{5,4},{6,7},{7,6},{8,9},{9,8},{10,11... | collective-permute-start | bytes 688136 | tf_op jit(solution)/shard_map/ppermute | solution.py:47
  97.8 13.1 %collective-permute-start.27 = (bf16[128,896]{1,0:T(8,128)(2,1)S(1)}, bf16[128,896]{1,0:T(8,128)(2,1)S(1)}, u32[]{:S(2)}, u32[]{:S(2)}) collective-permute-start(bf16[128,896]{1,0:T(8,128)(2,1)S(1)} %collective-permute-done.23.refs_4_), channel_id=1, source_target_pairs={{0,1},{1,0},{2,3},{3,2},{4,5},{5,4},{6,7},{7,6},{8,9},{9,8},{10,11... | collective-permute-start | bytes 688136 | tf_op jit(solution)/shard_map/ppermute | solution.py:47
  118.6 38.8 %all-to-all-start = ((bf16[32,32,1024]{2,1,0:T(8,128)(2,1)}), bf16[32,32,1024]{2,1,0:T(8,128)(2,1)S(1)}, u32[]{:S(2)}, u32[]{:S(2)}) async-start(bf16[32,32,1024]{2,1,0:T(8,128)(2,1)} %bitcast.6), calls=%async_computation | async-start | bytes 4194304 | tf_op jit(solution)/shard_map/all_to_all | solution.py:303
  (13 other events, 135.5 us)
